TPU v7x, 256 devices: a whole 4x4x8 slice. The times are simulated.
256 devices in a mesh: row: 32 (over z, y_lo, core), col: 8 (over x, y_hi).
Axes of the slice: x: 4, y: 4 (y_hi: 2, y_lo: 2; y = y_hi * 2 + y_lo), z: 8, core: 2. Of those that a mesh axis runs over, the one named last changes fastest.
Arguments:
- pair: bfloat16 [512, 512, 128], P('row', 'col'), may hold values from -6 to 6
- input_norm_gain: float32 [128], replicated, may hold values from 0.1 to 1.9
- input_norm_bias: float32 [128], replicated, may hold values from -3 to 3
- frozen_base_weight: float32 [128, 512], replicated, may hold values from -0.5 to 0.5
- adapter_down_factor: float32 [128, 16], replicated, may hold values from -0.6 to 0.6
- adapter_up_factor: float32 [16, 512], replicated, may hold values from -1.5 to 1.5
- magnitude: float32 [512], replicated, may hold values from 0.5 to 2
- output_gate_weight: bfloat16 [128, 128], replicated, may hold values from -0.5 to 0.5
- output_projection_weight: bfloat16 [128, 128], replicated, may hold values from -0.5 to 0.5
- centre_norm_gain: float32 [128], replicated, may hold values from 0.1 to 1.9
- centre_norm_bias: float32 [128], replicated, may hold values from -3 to 3
- cotangent: bfloat16 [512, 512, 128], P('row', 'col'), may hold values from -6 to 6
Outputs:
- update: bfloat16 [512, 512, 128], P('row', 'col')
- pair_input_gradient: bfloat16 [512, 512, 128], P('row', 'col')
- down_factor_gradient: float32 [128, 16], replicated
- up_factor_gradient: float32 [16, 512], replicated
- magnitude_vector_gradient: float32 [512], replicated
All inputs are finite; a program needn't handle non-finite values.
Results may differ from a plain program's by a relative error of at most 0.02.
Values may be sent and summed in bfloat16 or wider, within the bound.
A program may use at most 128 MiB of HBM per device.

v0:
```python
import jax
import jax.numpy as jnp
from jax import lax
from jax.sharding import PartitionSpec as P


def norm_parts(v):
    mean = jnp.mean(v, axis=-1, keepdims=True)
    centred = v - mean
    inv = lax.rsqrt(jnp.mean(centred * centred, axis=-1, keepdims=True) + 1e-05)
    return (centred * inv, inv)


def norm_back(grad_hat, zhat, inv):
    return inv * (
        grad_hat
        - jnp.mean(grad_hat, -1, keepdims=True)
        - zhat * jnp.mean(grad_hat * zhat, -1, keepdims=True)
    )


def chan_first(v):
    return jnp.transpose(v, (2, 0, 1))


def chan_last(v):
    return jnp.transpose(v, (1, 2, 0))


def on_device(
    pair,
    input_norm_gain,
    input_norm_bias,
    frozen_base_weight,
    adapter_down_factor,
    adapter_up_factor,
    magnitude,
    output_gate_weight,
    output_projection_weight,
    centre_norm_gain,
    centre_norm_bias,
    cotangent,
):
    single_float = jnp.float32
    highest_precision = lax.Precision.HIGHEST
    rows_here, cols_here, chans = pair.shape
    total_tokens = rows_here * lax.axis_size("row")
    zhat1, inv1 = norm_parts(pair.astype(single_float))
    zb = (zhat1 * input_norm_gain + input_norm_bias).astype(jnp.bfloat16)
    direction_matrix = frozen_base_weight + jnp.dot(
        adapter_down_factor,
        adapter_up_factor,
        precision=highest_precision,
        preferred_element_type=single_float,
    )
    column_norm = jnp.sqrt(jnp.sum(direction_matrix * direction_matrix, axis=0) + 1e-06)
    adapter_scale = magnitude / column_norm
    merged_weight_matrix = (direction_matrix * adapter_scale).astype(jnp.bfloat16)
    cells = zb.reshape(-1, chans)
    proj = jnp.dot(cells, merged_weight_matrix, preferred_element_type=single_float).reshape(
        rows_here, cols_here, 4 * chans
    )
    sig_a = jax.nn.sigmoid(proj[..., 0:chans])
    val_a = proj[..., chans : 2 * chans]
    sig_b = jax.nn.sigmoid(proj[..., 2 * chans : 3 * chans])
    val_b = proj[..., 3 * chans : 4 * chans]
    left = (sig_a * val_a).astype(jnp.bfloat16)
    right = (sig_b * val_b).astype(jnp.bfloat16)
    right_all = lax.all_gather(right, "row", axis=0, tiled=True)
    right_all_t = chan_first(right_all)
    left_t = chan_first(left)
    left_row = lax.all_gather(left, "col", axis=1, tiled=True)
    right_cols = lax.all_to_all(right_all, "col", split_axis=0, concat_axis=1, tiled=True)
    xsum_t = jnp.einsum(
        "cik,cjk->cij",
        chan_first(left_row),
        chan_first(right_cols),
        preferred_element_type=single_float,
    )
    xsum = chan_last(xsum_t)
    zhat2, inv2 = norm_parts(xsum)
    xb = (zhat2 * centre_norm_gain + centre_norm_bias).astype(jnp.bfloat16)
    gate = jax.nn.sigmoid(
        jnp.dot(cells, output_gate_weight, preferred_element_type=single_float)
    ).reshape(rows_here, cols_here, chans)
    outp = jnp.dot(
        xb.reshape(-1, chans), output_projection_weight, preferred_element_type=single_float
    ).reshape(rows_here, cols_here, chans)
    update = (gate * outp).astype(jnp.bfloat16)
    cot = cotangent.astype(single_float)
    egrad = (cot * gate).astype(jnp.bfloat16)
    dgp = (cot * outp * gate * (1.0 - gate)).astype(jnp.bfloat16)
    dxn = jnp.dot(
        egrad.reshape(-1, chans), output_projection_weight.T, preferred_element_type=single_float
    ).reshape(rows_here, cols_here, chans)
    dxb = norm_back(dxn * centre_norm_gain, zhat2, inv2).astype(jnp.bfloat16)
    dx_row = lax.all_gather(dxb, "col", axis=1, tiled=True)
    dx_row_t = chan_first(dx_row)
    dleft = chan_last(
        jnp.einsum("cij,cjk->cik", dx_row_t, right_all_t, preferred_element_type=single_float)
    )
    dright = lax.psum_scatter(
        chan_last(
            jnp.einsum("cij,cik->cjk", dx_row_t, left_t, preferred_element_type=single_float)
        ).astype(jnp.bfloat16),
        "row",
        scatter_dimension=0,
        tiled=True,
    ).astype(jnp.float32)
    dproj = jnp.concatenate(
        [
            dleft * val_a * sig_a * (1.0 - sig_a),
            dleft * sig_a,
            dright * val_b * sig_b * (1.0 - sig_b),
            dright * sig_b,
        ],
        axis=-1,
    ).astype(jnp.bfloat16)
    dproj_cells = dproj.reshape(-1, 4 * chans)
    dzb = jnp.dot(
        dproj_cells, merged_weight_matrix.T, preferred_element_type=single_float
    ) + jnp.dot(dgp.reshape(-1, chans), output_gate_weight.T, preferred_element_type=single_float)
    pair_input_gradient = norm_back(
        dzb.reshape(rows_here, cols_here, chans) * input_norm_gain, zhat1, inv1
    ).astype(jnp.bfloat16)
    local_weight = jnp.dot(cells.T, dproj_cells, preferred_element_type=single_float) / total_tokens
    triple_tensor = magnitude / (column_norm * column_norm * column_norm)
    merged_weight_gradient = lax.psum(local_weight, ("row", "col"))
    device_reduce_sum = jnp.sum(merged_weight_gradient * direction_matrix, axis=0)
    direction_gradient = merged_weight_gradient * adapter_scale - direction_matrix * (
        triple_tensor * device_reduce_sum
    )
    down_factor_gradient = jnp.dot(
        direction_gradient,
        adapter_up_factor.T,
        precision=highest_precision,
        preferred_element_type=single_float,
    )
    up_factor_gradient = jnp.dot(
        adapter_down_factor.T,
        direction_gradient,
        precision=highest_precision,
        preferred_element_type=single_float,
    )
    magnitude_vector_gradient = device_reduce_sum / column_norm
    return (
        update,
        pair_input_gradient,
        down_factor_gradient,
        up_factor_gradient,
        magnitude_vector_gradient,
    )


def solution(mesh):
    placed = (
        P("row", "col", None),
        P(),
        P(),
        P(),
        P(),
        P(),
        P(),
        P(),
        P(),
        P(),
        P(),
        P("row", "col", None),
    )
    return jax.shard_map(
        on_device,
        mesh=mesh,
        in_specs=placed,
        out_specs=(P("row", "col", None), P("row", "col", None), P(), P(), P()),
        check_vma=False,
    )
```

profile of v0, /device:TPU:1, one launch (start us, length us, event | category | flops | bytes accessed | tf_op | source)
XLA Modules:
  0.0 737.7 jit_solution(2998807988010905354)
XLA Ops:
  8.0 0.0 copy-start
  8.0 0.0 all-gather.6.cloned.1.call-start
  8.1 1.2 convert_reduce_fusion
  9.2 1.3 fusion.39
  10.6 1.4 multiply_reduce_fusion.5
  12.0 0.7 fusion.70
  12.7 1.3 fusion.34
  14.1 0.4 fusion.62
  14.5 1.1 multiply_convert_fusion.2
  15.5 0.0 all-gather.6.cloned.1.call-update
  15.6 0.0 copy-start.15
  15.6 76.6 %all-gather.6.cloned.1.call-done = bf16[512,64,128]{2,1,0:T(8,128)(2,1)} async-done(((bf16[16,64,128]{2,1,0:T(8,128)(2,1)}), bf16[512,64,128]{2,1,0:T(8,128)(2,1)}) %all-gather.6.cloned.1.call-update) | async-done | bytes 8388624 | tf_op jit(solution)/shard_map/all_gather | solution.py:69
  92.2 6.4 all-to-all-start
  98.7 0.0 all-gather.4.cloned.1.call-start
  98.7 0.5 all-gather.4.cloned.1.call-update
  99.2 0.0 all-gather.8.cloned.1.call-start
  99.3 0.3 fusion.12
  99.6 0.8 copy-done.3
  100.4 1.0 fusion.60
  101.4 1.5 copy.48
  103.0 115.8 %all-gather.4.cloned.1.call-done = bf16[16,512,128]{2,1,0:T(8,128)(2,1)} async-done(((bf16[16,64,128]{2,1,0:T(8,128)(2,1)}), bf16[16,512,128]{2,1,0:T(8,128)(2,1)}) %all-gather.4.cloned.1.call-update) | async-done | bytes 2097168 | tf_op jit(solution)/shard_map/all_gather | solution.py:72
  218.8 4.6 copy.46
  223.4 9.6 %copy.44 = bf16[64,8,64,128]{3,2,1,0:T(8,128)(2,1)} copy(bf16[64,8,64,128]{3,2,0,1:T(8,128)(2,1)} %bitcast.5) | data formatting | bytes 16777216 | tf_op jit(solution)/shard_map/all_to_all | solution.py:73
  233.0 12.6 %copy.45 = bf16[64,512,128]{1,0,2:T(8,128)(2,1)} copy(bf16[64,512,128]{2,1,0:T(8,128)(2,1)} %bitcast.75) | data formatting | bytes 16777216 | tf_op jit(solution)/shard_map/all_to_all | solution.py:73
  245.6 6.3 fusion.73
  251.9 0.2 multiply_reduce_fusion.1
  252.1 0.3 multiply_reduce_fusion.2
  252.5 0.1 copy-done.19
  252.6 1.4 multiply_convert_fusion
  254.0 2.3 copy.49
  256.3 0.0 all-gather.8.cloned.1.call-update
  256.3 0.2 reduce-scatter.2.cloned.1.call-start
  256.6 1.4 copy.53
  258.0 59.7 %all-gather.8.cloned.1.call-done = bf16[16,512,128]{2,0,1:T(8,128)(2,1)} async-done(((bf16[16,64,128]{2,0,1:T(8,128)(2,1)}), bf16[16,512,128]{2,0,1:T(8,128)(2,1)}) %all-gather.8.cloned.1.call-update) | async-done | bytes 2097168 | tf_op jit(solution)/shard_map/all_gather | solution.py:97
  317.7 4.9 copy.50
  322.6 7.2 fusion.4
  329.8 13.6 %copy.54 = bf16[128,512,64]{0,2,1:T(8,128)(2,1)} copy(bf16[128,512,64]{1,2,0:T(8,128)(2,1)} %fusion.4) | data formatting | bytes 16777216 | tf_op jit(solution)/shard_map/cij,cik->cjk/dot_general | solution.py:104
  343.4 0.0 reduce-scatter.2.cloned.1.call-update
  343.5 0.0 all-reduce.2.cloned.1.call-start
  343.5 13.6 %copy.51 = bf16[512,64,128]{0,1,2:T(8,128)(2,1)} copy(bf16[512,64,128]{2,1,0:T(8,128)(2,1)} %all-gather.6.cloned.1.call-done) | data formatting | bytes 16777216 | tf_op jit(solution)/shard_map/all_gather | solution.py:69
  357.1 2.1 fusion.43
  359.3 1.0 fusion.74
  360.3 5.7 fusion
  366.0 1.2 copy.52
  367.2 103.8 %reduce-scatter.2.cloned.1.call-done = bf16[16,64,128]{2,1,0:T(8,128)(2,1)} async-done(((bf16[512,64,128]{2,1,0:T(8,128)(2,1)}), bf16[16,64,128]{2,1,0:T(8,128)(2,1)}) %reduce-scatter.2.cloned.1.call-update) | async-done | bytes 262160 | tf_op jit(solution)/shard_map/reduce_scatter | solution.py:102
  471.0 1.6 fusion.56
  472.6 0.0 copy-start.11
  472.6 0.0 copy-start.17
  472.6 0.6 copy-done.10
  473.3 0.1 copy-done.11
  473.4 0.1 copy-done.12
  473.5 1.0 fusion.13
  474.5 0.0 all-reduce.2.cloned.1.call-update
  474.5 0.0 copy-start.2
  474.6 1.7 multiply_reduce_fusion.3
  476.2 0.0 copy-start.13
  476.3 0.5 fusion.35
  476.8 0.1 div.61
  476.9 1.3 fusion.38
  478.2 246.6 %all-reduce.2.cloned.1.call-done = f32[128,512]{1,0:T(8,128)} async-done(((f32[128,512]{1,0:T(8,128)}), f32[128,512]{1,0:T(8,128)}) %all-reduce.2.cloned.1.call-update) | async-done | bytes 262160 | tf_op jit(solution)/shard_map/psum | solution.py:128
  724.8 1.0 multiply_reduce_fusion.4
  725.8 0.6 fusion.69
  726.4 1.8 convolution_bitcast_fusion.1
  728.2 1.9 fusion.64
  (37 shorter events, 0.1 us)
Async XLA Ops:
  8.0 92.4 %copy-start = (bf16[128,128]{1,0:T(8,128)(2,1)S(1)}, bf16[128,128]{1,0:T(8,128)(2,1)}, u32[]{:S(2)}) copy-start(bf16[128,128]{1,0:T(8,128)(2,1)} %param.20) | copy-start | bytes 98308
  8.0 84.2 %all-gather.6.cloned.1.call-start = ((), (), s32[]{:S(2)}) async-start(), calls=%async_computation.3 | async-start | bytes 8650752 | tf_op jit(solution)/shard_map/all_gather | solution.py:69
  14.0 85.2 %copy-start.6 = (bf16[16,64,128]{2,1,0:T(8,128)(2,1)}, bf16[16,64,128]{2,1,0:T(8,128)(2,1)S(1)}, u32[]{:S(2)}) copy-start(bf16[16,64,128]{2,1,0:T(8,128)(2,1)S(1)} %fusion.34) | copy-start | bytes 786436
  15.6 83.7 %copy-start.15 = (bf16[128,128]{1,0:T(8,128)(2,1)S(1)}, bf16[128,128]{1,0:T(8,128)(2,1)}, u32[]{:S(2)}) copy-start(bf16[128,128]{1,0:T(8,128)(2,1)} %param.19) | copy-start | bytes 98308
  92.2 131.2 %all-to-all-start = ((bf16[512,64,128]{2,1,0:T(8,128)(2,1)}), bf16[512,64,128]{2,1,0:T(8,128)(2,1)}, u32[]{:S(2)}, u32[]{:S(2)}) async-start(bf16[512,64,128]{2,1,0:T(8,128)(2,1)} %all-gather.6.cloned.1.call-done), calls=%async_computation | async-start | bytes 16777216 | tf_op jit(solution)/shard_map/all_to_all | solution.py:73
  98.7 1.8 copy-start.8
  98.7 120.1 %all-gather.4.cloned.1.call-start = ((), (), s32[]{:S(2)}) async-start(), calls=%async_computation.2 | async-start | bytes 2359296 | tf_op jit(solution)/shard_map/all_gather | solution.py:72
  99.2 218.4 %all-gather.8.cloned.1.call-start = ((), (), s32[]{:S(2)}) async-start(), calls=%async_computation.4 | async-start | bytes 2359296 | tf_op jit(solution)/shard_map/all_gather | solution.py:97
  99.6 0.8 copy-start.3
  245.6 6.5 copy-start.18
  251.9 0.7 copy-start.19
  256.3 214.6 %reduce-scatter.2.cloned.1.call-start = ((), (), s32[]{:S(2)}) async-start(), calls=%async_computation.5 | async-start | bytes 8650752 | tf_op jit(solution)/shard_map/reduce_scatter | solution.py:102
  343.4 13.7 %copy-start.4 = (f32[1024,128]{1,0:T(8,128)S(1)}, f32[1024,128]{1,0:T(8,128)}, u32[]{:S(2)}) copy-start(f32[1024,128]{1,0:T(8,128)} %copy-done.3) | copy-start | bytes 1572868
  343.5 13.7 %copy-start.5 = (bf16[16,64,128]{1,0,2:T(8,128)(2,1)S(1)}, bf16[16,64,128]{1,0,2:T(8,128)(2,1)}, u32[]{:S(2)}) copy-start(bf16[16,64,128]{1,0,2:T(8,128)(2,1)} %get-tuple-element.16) | copy-start | bytes 786436
  343.5 381.3 %all-reduce.2.cloned.1.call-start = ((), (), s32[]{:S(2)}) async-start(), calls=%async_computation.6 | async-start | bytes 524288 | tf_op jit(solution)/shard_map/psum | solution.py:128
  357.1 3.2 copy-start.1
  367.2 106.3 %copy-start.7 = (bf16[16,64,128]{2,1,0:T(8,128)(2,1)S(1)}, bf16[16,64,128]{2,1,0:T(8,128)(2,1)}, u32[]{:S(2)}) copy-start(bf16[16,64,128]{2,1,0:T(8,128)(2,1)} %copy-done.6) | copy-start | bytes 786436
  472.6 0.7 copy-start.10
  472.6 0.8 copy-start.11
  472.6 0.9 copy-start.12
  472.6 1.9 copy-start.9
  472.6 1.9 copy-start.17
  474.5 1.7 copy-start.2
  476.2 249.6 %copy-start.16 = (f32[512]{0:T(512)S(1)}, f32[512]{0:T(512)}, u32[]{:S(2)}) copy-start(f32[512]{0:T(512)} %param.18) | copy-start | bytes 6148
  476.2 250.2 %copy-start.14 = (f32[128,16]{0,1:T(8,128)S(1)}, f32[128,16]{0,1:T(8,128)}, u32[]{:S(2)}) copy-start(f32[128,16]{0,1:T(8,128)} %param.16) | copy-start | bytes 24580
  476.2 252.0 %copy-start.13 = (f32[16,512]{1,0:T(8,128)S(1)}, f32[16,512]{1,0:T(8,128)}, u32[]{:S(2)}) copy-start(f32[16,512]{1,0:T(8,128)} %param.17) | copy-start | bytes 98308
Sparse Core Ops, SparseCore 0:
  15.7 76.4 all-gather.5
  343.6 127.3 reduce-scatter.1
Sparse Core Ops, SparseCore 1:
  102.3 116.4 all-gather.3
  256.4 61.2 all-gather.7
  474.6 250.1 all-reduce.1
where the time goes:
time: 740 us; the launch traced here: 738 us
  waiting for transfers between devices  603 us (81%)
  local copies, waits for them, and re-layouts  67.3 us (9%)
  matrix products  31.9 us (4%)
  between operations  16 us (2%)
  other arithmetic  12.6 us (2%)
    psum x1, waiting for transfers between devices, on_device(): merged_weight_gradient = lax.psum(local_weight, ('row', 'col'))  247 us
    all_gather x1, waiting for transfers between devices, on_device(): left_row = lax.all_gather(left, 'col', axis=1, tiled=True)  116 us
    reduce_scatter x1, waiting for transfers between devices, on_device(): lax.psum_scatter(chan_last(jnp.einsum('cij,cik->cjk', dx_row_t, left_t, p...  104 us
    all_gather x1, waiting for transfers between devices, on_device(): right_all = lax.all_gather(right, 'row', axis=0, tiled=True)  76.6 us
    all_gather x1, waiting for transfers between devices, on_device(): dx_row = lax.all_gather(dxb, 'col', axis=1, tiled=True)  59.7 us
    all_to_all x2, local copies, waits for them, and re-layouts, on_device(): lax.all_to_all(right_all, 'col', split_axis=0, concat_axis=1, tiled=True)  22.2 us
  transfers between devices with their start and end apart: 6, of which 5 were waited for; matrix products, arithmetic and copies ran while one was open for 5% of the time, Pallas kernels for 0%

commit v1 on v0

v1 whole, which is shorter than its diff:
```python
import jax
import jax.numpy as jnp
from jax import lax
from jax.experimental import pallas as pl
from jax.experimental.pallas import tpu as pltpu
from jax.sharding import PartitionSpec as P

MESH = pl.DeviceIdType.MESH
F32 = jnp.float32
BF16 = jnp.bfloat16
NZ, NY, NX = 8, 4, 4
CH = 128
TOKENS = 512
HIGHEST = lax.Precision.HIGHEST


def dot(a, b, ca=1, cb=0, precision=None):
    return lax.dot_general(
        a, b, (((ca,), (cb,)), ((), ())), precision=precision, preferred_element_type=F32
    )


def far_first(k, n):
    return n // 2 + (1 - 2 * lax.rem(k, 2)) * lax.div(k + 1, 2)


def low_half(shape):
    return lax.broadcasted_iota(jnp.int32, shape, 1) < 64


def pair_up(first, second):
    low = low_half(first.shape)
    return (
        jnp.where(low, first, pltpu.roll(second, 64, 1)),
        jnp.where(low, pltpu.roll(first, 64, 1), second),
    )


def column(row_ref):
    n = row_ref.shape[1]
    return jnp.transpose(jnp.broadcast_to(row_ref[...], (128, n)))


def kernel(
    pair,
    gain1,
    bias1,
    base,
    down,
    up,
    mag,
    wg,
    wo,
    gain2,
    bias2,
    cot,
    update,
    pig,
    gdown,
    gup,
    gmag,
    s1,
    r1,
    s2,
    r2,
    s3,
    r3,
    s4,
    r4,
    amat,
    bmat,
    dbsend,
    dbrecv,
    big,
    mid,
    half,
    dbs,
    sa,
    va,
    sb,
    vb,
    zhat1,
    inv1,
    zbt,
    gate,
    cott,
    dgp,
    dproj,
    vmat,
    wmat,
    wmat_t,
    gain1c,
    gain2c,
    bias2c,
    parts,
    level1,
    level2,
    whole,
    ssem,
    rsem,
    sibsem,
    redsem,
):
    row = lax.axis_index("row")
    q = lax.axis_index("col")
    m = lax.div(row, 2)
    h = lax.rem(row, 2)
    z = lax.div(m, 2)
    x = lax.div(q, 2)
    y = lax.rem(q, 2) * 2 + lax.rem(m, 2)
    me = m * 8 + q
    sibling = (m * 2 + 1 - h, q)

    def chip_at(dz, dy, dx):
        z2 = lax.rem(z + dz, NZ)
        y2 = lax.rem(y + dy, NY)
        x2 = lax.rem(x + dx, NX)
        return z2 * 2 + lax.rem(y2, 2), x2 * 2 + lax.div(y2, 2)

    def chip_by(t):
        return chip_at(
            far_first(lax.div(t, 16), NZ),
            far_first(lax.rem(lax.div(t, 4), 4), NY),
            far_first(lax.rem(t, 4), NX),
        )

    barrier = pltpu.get_barrier_semaphore()

    def greet(t, carry):
        m2, q2 = chip_by(t)
        pl.semaphore_signal(barrier, inc=1, device_id=(m2 * 2 + h, q2), device_id_type=MESH)
        return carry

    lax.fori_loop(0, 127, greet, 0)

    def greet_other(t, carry):
        m2, q2 = chip_at(t, 0, 0)
        pl.semaphore_signal(barrier, inc=1, device_id=(m2 * 2 + 1 - h, q2), device_id_type=MESH)
        return carry

    lax.fori_loop(0, NZ, greet_other, 0)

    v = base[...] + dot(down[...], up[...], precision=HIGHEST)
    nrm = jnp.sqrt(jnp.sum(v * v, axis=0, keepdims=True) + 1e-06)
    scale = mag[...] / nrm
    vmat[...] = v
    w = (v * scale).astype(BF16)
    wmat[...] = w
    wmat_t[...] = jnp.transpose(w.astype(F32)).astype(BF16)
    wg_t = jnp.transpose(wg[...].astype(F32)).astype(BF16)
    gain1c[...] = column(gain1)
    bias1c = column(bias1)
    gain2c[...] = column(gain2)
    bias2c[...] = column(bias2)

    for s in range(8):
        lanes = pl.ds(s * 128, 128)
        zs = jnp.concatenate([pair[s], pair[8 + s]], axis=0).astype(F32)
        zs = jnp.transpose(zs)
        mean = jnp.mean(zs, axis=0, keepdims=True)
        centred = zs - mean
        inv = lax.rsqrt(jnp.mean(centred * centred, axis=0, keepdims=True) + 1e-05)
        zh = centred * inv
        zhat1[:, lanes] = zh
        inv1[:, lanes] = inv
        zb = (zh * gain1c[...] + bias1c).astype(BF16)
        zbt[:, lanes] = zb
        proj = dot(wmat_t[...], zb)
        sig_a = jax.nn.sigmoid(proj[0:128])
        sig_b = jax.nn.sigmoid(proj[256:384])
        sa[:, lanes] = sig_a
        va[:, lanes] = proj[128:256]
        sb[:, lanes] = sig_b
        vb[:, lanes] = proj[384:512]
        big[pl.ds(s, CH, stride=16), :] = sig_a * proj[128:256]
        big[pl.ds(8 + s, CH, stride=16), :] = sig_b * proj[384:512]
    s1[...] = big[...].reshape(CH, 16, 128).astype(BF16)

    pl.semaphore_wait(barrier, 127 + NZ)

    def exchange(step, src, dst_slot):
        local = pltpu.make_async_copy(src(m, q), dst_slot, rsem.at[step])
        local.start()

        def send(t, carry):
            m2, q2 = chip_by(t)
            pltpu.make_async_remote_copy(
                src_ref=src(m2, q2),
                dst_ref=dst_slot,
                send_sem=ssem.at[step],
                recv_sem=rsem.at[step],
                device_id=(m2 * 2 + h, q2),
                device_id_type=MESH,
            ).start()
            return carry

        lax.fori_loop(0, 127, send, 0)

    def arrived(step, ref):
        pltpu.make_async_copy(ref, ref, rsem.at[step]).wait()

    def sent(step, ref):
        pltpu.make_async_copy(ref, ref, ssem.at[step]).wait()

    exchange(0, lambda m2, q2: s1.at[m2 * 8 + q2], r1.at[q, m])

    for s in range(8):
        lanes = pl.ds(s * 128, 128)
        gate[:, lanes] = jax.nn.sigmoid(dot(wg_t, zbt[:, lanes]))
        cs = jnp.concatenate([cot[s], cot[8 + s]], axis=0).astype(F32)
        cott[:, lanes] = jnp.transpose(cs)

    arrived(0, r1)

    for p in range(4):
        lanes = pl.ds(p * 128, 128)
        first = r1[2 * p].astype(F32)
        second = r1[2 * p + 1].astype(F32)
        for part in range(2):
            rows = slice(part * 8, part * 8 + 8)
            even, odd = pair_up(
                first[:, rows, :].reshape(128, 128), second[:, rows, :].reshape(128, 128)
            )
            target = half if part == 0 else mid
            target[:, 0:8, lanes] = even.reshape(16, 8, 128)
            target[:, 8:16, lanes] = odd.reshape(16, 8, 128)
    bmat[:, pl.ds(h, 1)] = mid[...].astype(BF16).reshape(16, 1, 16, TOKENS)
    bcopy = pltpu.make_async_remote_copy(
        src_ref=bmat.at[:, h],
        dst_ref=bmat.at[:, h],
        send_sem=sibsem.at[0],
        recv_sem=sibsem.at[1],
        device_id=sibling,
        device_id_type=MESH,
    )
    bcopy.start()
    amat[...] = half[...].reshape(256, TOKENS).astype(BF16)
    bcopy.wait()

    def split(value, p):
        first, second = pair_up(
            value[:, 0:8, :].reshape(128, 128), value[:, 8:16, :].reshape(128, 128)
        )
        return first.reshape(16, 8, 128), second.reshape(16, 8, 128)

    ball = bmat[...].reshape(TOKENS, TOKENS)
    xs = dot(amat[...], ball, 1, 1)
    for p in range(4):
        block = xs[:, p * 128 : (p + 1) * 128].reshape(16, 16, 128)
        first, second = split(block, p)
        s2[2 * p] = first.astype(BF16)
        s2[2 * p + 1] = second.astype(BF16)
    exchange(1, lambda m2, q2: s2.at[q2, m2], r2.at[me])
    arrived(1, r2)

    big[0:1024] = r2[...].astype(F32).reshape(1024, 128)
    wo_t = jnp.transpose(wo[...].astype(F32)).astype(BF16)
    for s in range(8):
        lanes = pl.ds(s * 128, 128)
        xsl = big[pl.ds(s, CH, stride=8), :]
        mean = jnp.mean(xsl, axis=0, keepdims=True)
        centred = xsl - mean
        inv = lax.rsqrt(jnp.mean(centred * centred, axis=0, keepdims=True) + 1e-05)
        xhat = centred * inv
        xb = (xhat * gain2c[...] + bias2c[...]).astype(BF16)
        outp = dot(wo_t, xb)
        g = gate[:, lanes]
        c = cott[:, lanes]
        up_cells = jnp.transpose(g * outp).astype(BF16)
        update[s] = up_cells[0:64]
        update[8 + s] = up_cells[64:128]
        e = (c * g).astype(BF16)
        dgp[:, lanes] = (c * outp * g * (1.0 - g)).astype(BF16)
        dxh = dot(wo[...], e) * gain2c[...]
        dx = inv * (
            dxh
            - jnp.mean(dxh, axis=0, keepdims=True)
            - xhat * jnp.mean(dxh * xhat, axis=0, keepdims=True)
        )
        big[pl.ds(1024 + s, CH, stride=8), :] = dx
    s3[...] = big[1024:2048].reshape(CH, 8, 128).astype(BF16)
    exchange(2, lambda m2, q2: s3.at[m2 * 8 + q2], r3.at[q, m])
    arrived(2, r3)

    for p in range(4):
        lanes = pl.ds(p * 128, 128)
        even, odd = pair_up(
            r3[2 * p].astype(F32).reshape(128, 128), r3[2 * p + 1].astype(F32).reshape(128, 128)
        )
        half[:, 0:8, lanes] = even.reshape(16, 8, 128)
        half[:, 8:16, lanes] = odd.reshape(16, 8, 128)
    dxm = half[...].reshape(256, TOKENS)
    dxm_t = jnp.transpose(dxm).astype(BF16)
    dbs[...] = dot(dxm_t, amat[...]).reshape(16, 2, 16, TOKENS)
    dbsend[...] = dbs[:, pl.ds(1 - h, 1)].reshape(16, 16, TOKENS).astype(BF16)
    dcopy = pltpu.make_async_remote_copy(
        src_ref=dbsend,
        dst_ref=dbrecv,
        send_sem=sibsem.at[2],
        recv_sem=sibsem.at[3],
        device_id=sibling,
        device_id_type=MESH,
    )
    dcopy.start()
    half[...] = dot(dxm.astype(BF16), bmat[...].reshape(TOKENS, TOKENS)).reshape(16, 16, TOKENS)
    dcopy.wait()
    mid[...] = dbs[:, pl.ds(h, 1)].reshape(16, 16, TOKENS) + dbrecv[...].astype(F32)
    for p in range(4):
        lanes = pl.ds(p * 128, 128)
        a0, a1 = split(half[:, :, lanes], p)
        b0, b1 = split(mid[:, :, lanes], p)
        s4[2 * p] = jnp.concatenate([a0, b0], axis=1).astype(BF16)
        s4[2 * p + 1] = jnp.concatenate([a1, b1], axis=1).astype(BF16)
    exchange(3, lambda m2, q2: s4.at[q2, m2], r4.at[me])
    arrived(3, r4)

    big[...] = r4[...].astype(F32).reshape(2048, 128)
    for s in range(8):
        lanes = pl.ds(s * 128, 128)
        das = big[pl.ds(s, CH, stride=16), :]
        dbl = big[pl.ds(8 + s, CH, stride=16), :]
        sig_a = sa[:, lanes]
        sig_b = sb[:, lanes]
        dproj[0:128, lanes] = (das * va[:, lanes] * sig_a * (1.0 - sig_a)).astype(BF16)
        dproj[128:256, lanes] = (das * sig_a).astype(BF16)
        dproj[256:384, lanes] = (dbl * vb[:, lanes] * sig_b * (1.0 - sig_b)).astype(BF16)
        dproj[384:512, lanes] = (dbl * sig_b).astype(BF16)

    dw = dot(zbt[...], dproj[...], 1, 1) * (1.0 / TOKENS)
    v = vmat[...]
    nrm = jnp.sqrt(jnp.sum(v * v, axis=0, keepdims=True) + 1e-06)
    scale = mag[...] / nrm
    p_sum = jnp.sum(dw * v, axis=0, keepdims=True)
    dv = dw * scale - v * (mag[...] * p_sum / (nrm * nrm * nrm))
    down_t = jnp.transpose(down[...])
    gd = dot(up[...], dv, 1, 1, precision=HIGHEST)
    gu = dot(down_t, dv, precision=HIGHEST)
    gm = p_sum / nrm
    parts[0] = gd[0:8]
    parts[1] = gd[8:16]
    for p in range(4):
        parts[2 + 2 * p] = gu[0:8, p * 128 : (p + 1) * 128]
        parts[3 + 2 * p] = gu[8:16, p * 128 : (p + 1) * 128]
        parts[10, p : p + 1] = gm[:, p * 128 : (p + 1) * 128]
    parts[10, 4:8] = jnp.zeros((4, 128), F32)
    parts[11:16] = jnp.zeros((5, 8, 128), F32)

    g_me = z * 2 + h
    f_me = y * 4 + x

    def in_column(g):
        z2 = lax.div(g, 2)
        return (z2 * 2 + lax.rem(m, 2)) * 2 + lax.rem(g, 2), q

    def in_plane(f):
        y2 = lax.div(f, 4)
        x2 = lax.rem(f, 4)
        return (z * 2 + lax.rem(y2, 2)) * 2 + h, x2 * 2 + lax.div(y2, 2)

    def spread(step, own, src, dst, where):
        local = pltpu.make_async_copy(src(own), dst, redsem.at[step, 1])
        local.start()

        def send(t, carry):
            other = lax.rem(own + t, 16)
            pltpu.make_async_remote_copy(
                src_ref=src(other),
                dst_ref=dst,
                send_sem=redsem.at[step, 0],
                recv_sem=redsem.at[step, 1],
                device_id=where(other),
                device_id_type=MESH,
            ).start()
            return carry

        lax.fori_loop(1, 16, send, 0)

    def gathered(step, ref):
        pltpu.make_async_copy(ref, ref, redsem.at[step, 1]).wait()

    spread(0, g_me, lambda g: parts.at[g], level1.at[g_me], in_column)

    def pair_gradient(s):
        lanes = pl.ds(s * 128, 128)
        dzb = dot(wmat[...], dproj[:, lanes]) + dot(wg[...], dgp[:, lanes])
        dzh = dzb * gain1c[...]
        zh = zhat1[:, lanes]
        dz = inv1[:, lanes] * (
            dzh
            - jnp.mean(dzh, axis=0, keepdims=True)
            - zh * jnp.mean(dzh * zh, axis=0, keepdims=True)
        )
        cells = jnp.transpose(dz).astype(BF16)
        pig[s] = cells[0:64]
        pig[8 + s] = cells[64:128]

    for s in range(0, 4):
        pair_gradient(s)
    gathered(0, level1)
    level1[0] = jnp.sum(level1[...], axis=0)
    spread(1, f_me, lambda f: level1.at[0], level2.at[f_me], in_plane)
    for s in range(4, 8):
        pair_gradient(s)
    gathered(1, level2)
    level2[0] = jnp.sum(level2[...], axis=0)
    spread(2, g_me, lambda g: level2.at[0], whole.at[g_me], in_column)
    gathered(2, whole)

    gdown[...] = jnp.transpose(whole[0:2].reshape(16, 128))
    for p in range(4):
        gup[:, p * 128 : (p + 1) * 128] = whole[2 + 2 * p : 4 + 2 * p].reshape(16, 128)
        gmag[:, p * 128 : (p + 1) * 128] = whole[10, p : p + 1]

    sent(0, s1.at[0:127])
    sent(1, r2.at[0:127])
    sent(2, s3.at[0:127])
    sent(3, r4.at[0:127])
    for step in range(3):
        pltpu.make_async_copy(
            parts.at[0:15], parts.at[0:15], redsem.at[step, 0]
        ).wait()


def on_device(
    pair,
    input_norm_gain,
    input_norm_bias,
    frozen_base_weight,
    adapter_down_factor,
    adapter_up_factor,
    magnitude,
    output_gate_weight,
    output_projection_weight,
    centre_norm_gain,
    centre_norm_bias,
    cotangent,
):
    vmem = pl.BlockSpec(memory_space=pltpu.VMEM)
    cells = (CH, 1024)
    update, pig, gdown, gup, gmag = pl.pallas_call(
        kernel,
        out_shape=(
            jax.ShapeDtypeStruct(pair.shape, BF16),
            jax.ShapeDtypeStruct(pair.shape, BF16),
            jax.ShapeDtypeStruct((CH, 16), F32),
            jax.ShapeDtypeStruct((16, 4 * CH), F32),
            jax.ShapeDtypeStruct((1, 4 * CH), F32),
        ),
        in_specs=[vmem] * 12,
        out_specs=(vmem,) * 5,
        scratch_shapes=[
            pltpu.VMEM((CH, 16, 128), BF16),
            pltpu.VMEM((8, 16, 16, 128), BF16),
            pltpu.VMEM((8, 16, 8, 128), BF16),
            pltpu.VMEM((CH, 8, 128), BF16),
            pltpu.VMEM((CH, 8, 128), BF16),
            pltpu.VMEM((8, 16, 8, 128), BF16),
            pltpu.VMEM((8, 16, 16, 128), BF16),
            pltpu.VMEM((CH, 16, 128), BF16),
            pltpu.VMEM((256, TOKENS), BF16),
            pltpu.VMEM((16, 2, 16, TOKENS), BF16),
            pltpu.VMEM((16, 16, TOKENS), BF16),
            pltpu.VMEM((16, 16, TOKENS), BF16),
            pltpu.VMEM((2048, 128), F32),
            pltpu.VMEM((16, 16, TOKENS), F32),
            pltpu.VMEM((16, 16, TOKENS), F32),
            pltpu.VMEM((16, 2, 16, TOKENS), F32),
            pltpu.VMEM(cells, F32),
            pltpu.VMEM(cells, F32),
            pltpu.VMEM(cells, F32),
            pltpu.VMEM(cells, F32),
            pltpu.VMEM(cells, F32),
            pltpu.VMEM((1, 1024), F32),
            pltpu.VMEM(cells, BF16),
            pltpu.VMEM(cells, F32),
            pltpu.VMEM(cells, F32),
            pltpu.VMEM(cells, BF16),
            pltpu.VMEM((4 * CH, 1024), BF16),
            pltpu.VMEM((CH, 4 * CH), F32),
            pltpu.VMEM((CH, 4 * CH), BF16),
            pltpu.VMEM((4 * CH, CH), BF16),
            pltpu.VMEM((CH, 128), F32),
            pltpu.VMEM((CH, 128), F32),
            pltpu.VMEM((CH, 128), F32),
            pltpu.VMEM((16, 8, 128), F32),
            pltpu.VMEM((16, 8, 128), F32),
            pltpu.VMEM((16, 8, 128), F32),
            pltpu.VMEM((16, 8, 128), F32),
            pltpu.SemaphoreType.DMA((4,)),
            pltpu.SemaphoreType.DMA((4,)),
            pltpu.SemaphoreType.DMA((4,)),
            pltpu.SemaphoreType.DMA((3, 2)),
        ],
        compiler_params=pltpu.CompilerParams(
            collective_id=0, has_side_effects=True, vmem_limit_bytes=48 * 2**20
        ),
    )(
        pair,
        input_norm_gain.reshape(1, CH),
        input_norm_bias.reshape(1, CH),
        frozen_base_weight,
        adapter_down_factor,
        adapter_up_factor,
        magnitude.reshape(1, 4 * CH),
        output_gate_weight,
        output_projection_weight,
        centre_norm_gain.reshape(1, CH),
        centre_norm_bias.reshape(1, CH),
        cotangent,
    )
    return update, pig, gdown, gup, gmag.reshape(4 * CH)


def solution(mesh):
    cells = P("row", "col", None)
    placed = (cells,) + (P(),) * 10 + (cells,)
    return jax.shard_map(
        on_device,
        mesh=mesh,
        in_specs=placed,
        out_specs=(cells, cells, P(), P(), P()),
        check_vma=False,
    )
```

time: 740 us -> 97.7 us (0.13)
  waiting for transfers between devices: 603 us -> 0 us
  Pallas kernels: 0 us -> 88.3 us
  local copies, waits for them, and re-layouts: 67.3 us -> 8.31 us
  matrix products: 31.9 us -> 0 us
  between operations: 16 us -> 0.71 us
  other arithmetic: 12.6 us -> 0 us
    all_gather x3 -> x0, waiting for transfers between devices: 252 us -> none  [the longest x1 116 us: on_device(): left_row = lax.all_gather(left, 'col', axis=1, tiled=True)]
    psum x1 -> x0, waiting for transfers between devices: 247 us -> none  [on_device(): merged_weight_gradient = lax.psum(local_weight, ('row', 'col'))]
    reduce_scatter x1 -> x0, waiting for transfers between devices: 104 us -> none  [on_device(): lax.psum_scatter(chan_last(jnp.einsum('cij,cik->cjk', dx_row_t, left_t, p...]
    pallas_call x0 -> x1, Pallas kernels: none -> 88.3 us  [on_device(): pl.pallas_call(kernel, out_shape=(jax.ShapeDtypeStruct(pair.shape, BF16),...]
    dot_general x13 -> x0, matrix products: 31.9 us -> none  [the longest x1 7.19 us: on_device(): jnp.einsum('cij,cik->cjk', dx_row_t, left_t, preferred_element_type=singl...]
    all_to_all x2 -> x0, local copies, waits for them, and re-layouts: 22.2 us -> none  [on_device(): lax.all_to_all(right_all, 'col', split_axis=0, concat_axis=1, tiled=True)]
    all_gather x2 -> x0, local copies, waits for them, and re-layouts: 18.5 us -> none  [the longest x1 13.6 us: on_device(): right_all = lax.all_gather(right, 'row', axis=0, tiled=True)]
    dot_general x3 -> x0, local copies, waits for them, and re-layouts: 16.4 us -> none  [the longest x1 13.6 us: on_device(): jnp.einsum('cij,cik->cjk', dx_row_t, left_t, preferred_element_type=singl...]
  transfers between devices with their start and end apart: 6 -> 0, of which waited for: 5 -> 0; matrix products, arithmetic and copies ran while one was open for 5% -> 0% of each run, Pallas kernels for 0% -> 0%
where the time goes in v1:
time: 97.7 us; the launch traced here: 97.3 us
  Pallas kernels  88.3 us (90%)
  local copies, waits for them, and re-layouts  8.31 us (9%)
    pallas_call x1, Pallas kernels, on_device(): pl.pallas_call(kernel, out_shape=(jax.ShapeDtypeStruct(pair.shape, BF16),...  88.3 us
    unnamed x30, local copies, waits for them, and re-layouts  8.31 us

profile of v1, /device:TPU:1, one launch (start us, length us, event | category | flops | bytes accessed | tf_op | source)
XLA Modules:
  0.0 97.3 jit_solution(18081981758128978472)
XLA Ops:
  0.6 0.0 copy-start.11
  0.6 0.7 copy-done.11
  1.3 0.0 copy-start.3
  1.3 0.0 copy-start.4
  1.3 0.0 copy-start.6
  1.3 0.0 copy-start.7
  1.3 0.0 copy-start.8
  1.4 0.0 copy-start.9
  1.4 0.0 copy-start.10
  1.4 0.1 copy.17.down
  1.5 0.6 copy-done.3
  2.1 0.0 copy-done.4
  2.1 0.0 copy-done.6
  2.1 0.0 copy-done.7
  2.1 0.0 copy-done.8
  2.1 0.0 copy-done.9
  2.1 0.0 copy-done.10
  2.1 0.0 copy-start
  2.1 0.9 copy-done
  3.1 0.0 copy-start.1
  3.1 0.9 copy-done.1
  4.0 0.0 copy-start.2
  4.0 0.9 copy-done.2
  5.0 0.0 copy-start.5
  5.0 0.8 copy-done.5
  5.7 88.3 %shard_map.155 = (bf16[16,64,128]{2,1,0:T(8,128)(2,1)S(1)}, bf16[16,64,128]{2,1,0:T(8,128)(2,1)S(1)}, f32[128,16]{1,0:T(8,128)S(1)}, f32[16,512]{1,0:T(8,128)S(1)}, f32[1,512]{1,0:T(1,128)S(1)}) custom-call(bf16[16,64,128]{2,1,0:T(8,128)(2,1)S(1)} %copy-done, f32[1,128]{1,0:T(1,128)S(1)} %bitcast.8, f32[1,128]{1,0:T(1,128)S(1)} %bitcast.9, ...), custom_call_target="tpu_custom_call" | custom-call | tf_op jit(solution)/shard_map/pallas_call | solution.py:440
  94.0 0.7 copy.18
  94.7 0.7 copy.23
  95.4 0.7 copy.24
  96.1 0.6 copy.25
  96.7 0.6 copy.26
Async XLA Ops:
  0.6 0.7 copy-start.11
  1.3 0.8 copy-start.3
  1.3 0.8 copy-start.4
  1.3 0.8 copy-start.6
  1.3 0.8 copy-start.7
  1.3 0.8 copy-start.8
  1.4 0.8 copy-start.9
  1.4 0.8 copy-start.10
  2.1 1.0 copy-start
  3.1 0.9 copy-start.1
  4.0 0.9 copy-start.2
  5.0 0.8 copy-start.5

commit v2 on v1

v2 whole, which is shorter than its diff:
```python
import jax
import jax.numpy as jnp
from jax import lax
from jax.experimental import pallas as pl
from jax.experimental.pallas import tpu as pltpu
from jax.sharding import PartitionSpec as P

MESH = pl.DeviceIdType.MESH
F32 = jnp.float32
BF16 = jnp.bfloat16
NZ, NY, NX = 8, 4, 4
CH = 128
TOKENS = 512
VMEM_GRANT = 63 * 2**20
HIGHEST = lax.Precision.HIGHEST
FAR_Z = (4, 3, 5, 2, 6, 1, 7, 0)
FAR_PLANE = sorted(
    ((dy, dx) for dy in range(NY) for dx in range(NX)),
    key=lambda o: -(min(o[0], NY - o[0]) + min(o[1], NX - o[1])),
)
FAR_COLUMN = sorted(
    ((dz, dh) for dz in range(NZ) for dh in range(2)),
    key=lambda o: -(2 * min(o[0], NZ - o[0]) + o[1]),
)


def dot(a, b, ca=1, cb=0, precision=None):
    return lax.dot_general(
        a, b, (((ca,), (cb,)), ((), ())), precision=precision, preferred_element_type=F32
    )


def far_first(k, n):
    return n // 2 + (1 - 2 * lax.rem(k, 2)) * lax.div(k + 1, 2)


def low_half(shape):
    return lax.broadcasted_iota(jnp.int32, shape, 1) < 64


def pair_up(first, second):
    low = low_half(first.shape)
    return (
        jnp.where(low, first, pltpu.roll(second, 64, 1)),
        jnp.where(low, pltpu.roll(first, 64, 1), second),
    )


def column(row_ref):
    n = row_ref.shape[1]
    return jnp.transpose(jnp.broadcast_to(row_ref[...], (128, n)))


def kernel(*refs):
    operands, (update_out, pig_out, whole), scratch = refs[:12], refs[12:15], refs[15:]
    (
        pair,
        gain1,
        bias1,
        base,
        down_t,
        up,
        mag,
        wg,
        wo,
        gain2,
        bias2,
        cot,
        update,
        pig,
        s1a,
        s1b,
        r1a,
        r1b,
        s2,
        r2,
        s3,
        r3,
        s4a,
        s4b,
        r4a,
        r4b,
        amat,
        bmat,
        dbsend,
        dbrecv,
        big_a,
        big_b,
        mid,
        half,
        dbs,
        sa,
        va,
        sb,
        vb,
        zhat1,
        inv1,
        zbt,
        gate,
        cott,
        dgp,
        dproj,
        vmat,
        wmat,
        wmat_t,
        gain1c,
        gain2c,
        bias2c,
        parts,
        level1,
        level2,
        ssem,
        rsem,
        sibsem,
        redsem,
        insem,
        outsem,
    ) = scratch
    local = (pair, gain1, bias1, base, down_t, up, mag, wg, wo, gain2, bias2, cot)
    row = lax.axis_index("row")
    q = lax.axis_index("col")
    m = lax.div(row, 2)
    h = lax.rem(row, 2)
    z = lax.div(m, 2)
    x = lax.div(q, 2)
    y = lax.rem(q, 2) * 2 + lax.rem(m, 2)
    me = m * 8 + q
    sibling = (m * 2 + 1 - h, q)

    def chip_at(dz, dy, dx):
        z2 = lax.rem(z + dz, NZ)
        y2 = lax.rem(y + dy, NY)
        x2 = lax.rem(x + dx, NX)
        return z2 * 2 + lax.rem(y2, 2), x2 * 2 + lax.div(y2, 2)

    z_rows = [4 * lax.rem(z + dz, NZ) + h for dz in FAR_Z]

    def plane(t):
        y2 = lax.rem(y + far_first(lax.div(t, 4), NY), NY)
        x2 = lax.rem(x + far_first(lax.rem(t, 4), NX), NX)
        return 2 * lax.rem(y2, 2), x2 * 2 + lax.div(y2, 2)

    def to_all(act):
        def over_plane(t, carry):
            parity, q2 = plane(t)
            for z_row in z_rows:
                act(z_row + parity, q2)
            return carry

        lax.fori_loop(0, 15, over_plane, 0)
        parity, q2 = plane(15)
        for z_row in z_rows[:-1]:
            act(z_row + parity, q2)

    barrier = pltpu.get_barrier_semaphore()

    def greet(row2, q2):
        pl.semaphore_signal(barrier, inc=1, device_id=(row2, q2), device_id_type=MESH)

    to_all(greet)
    for z_row in z_rows:
        greet(z_row + 2 * lax.rem(y, 2) + 1 - 2 * h, q)

    loads = [
        pltpu.make_async_copy(operand, here, insem.at[n])
        for n, (operand, here) in enumerate(zip(operands, local))
    ]
    for load in loads:
        load.start()
    for load in loads:
        load.wait()
    pending = []

    def finish():
        for wait in pending:
            wait()

    v = base[...] + dot(down_t[...], up[...], 0, 0, precision=HIGHEST)
    nrm = jnp.sqrt(jnp.sum(v * v, axis=0, keepdims=True) + 1e-06)
    scale = mag[...] / nrm
    vmat[...] = v
    w = (v * scale).astype(BF16)
    wmat[...] = w
    wmat_t[...] = jnp.transpose(w.astype(F32)).astype(BF16)
    wg_t = jnp.transpose(wg[...].astype(F32)).astype(BF16)
    gain1c[...] = column(gain1)
    bias1c = column(bias1)
    gain2c[...] = column(gain2)
    bias2c[...] = column(bias2)

    for s in range(8):
        lanes = pl.ds(s * 128, 128)
        zs = jnp.concatenate([pair[s], pair[8 + s]], axis=0).astype(F32)
        zs = jnp.transpose(zs)
        mean = jnp.mean(zs, axis=0, keepdims=True)
        centred = zs - mean
        inv = lax.rsqrt(jnp.mean(centred * centred, axis=0, keepdims=True) + 1e-05)
        zh = centred * inv
        zhat1[:, lanes] = zh
        inv1[:, lanes] = inv
        zb = (zh * gain1c[...] + bias1c).astype(BF16)
        zbt[:, lanes] = zb
        proj = dot(wmat_t[...], zb)
        sig_a = jax.nn.sigmoid(proj[0:128])
        sig_b = jax.nn.sigmoid(proj[256:384])
        sa[:, lanes] = sig_a
        va[:, lanes] = proj[128:256]
        sb[:, lanes] = sig_b
        vb[:, lanes] = proj[384:512]
        big_a[pl.ds(s, CH, stride=8), :] = sig_a * proj[128:256]
        big_b[pl.ds(s, CH, stride=8), :] = sig_b * proj[384:512]
    s1b[...] = big_b[...].reshape(CH, 8, 128).astype(BF16)
    s1a[...] = big_a[...].reshape(CH, 8, 128).astype(BF16)

    pl.semaphore_wait(barrier, 127 + NZ)

    def exchange(step, src, dst_slot, received):
        own = pltpu.make_async_copy(src(m, q), dst_slot, rsem.at[step])
        own.start()

        def send(row2, q2):
            pltpu.make_async_remote_copy(
                src_ref=src(lax.div(row2, 2), q2),
                dst_ref=dst_slot,
                send_sem=ssem.at[step],
                recv_sem=rsem.at[step],
                device_id=(row2, q2),
                device_id_type=MESH,
            ).start()

        to_all(send)
        others = s1a.at[0:127]
        pending.append(pltpu.make_async_copy(others, others, ssem.at[step]).wait)
        return pltpu.make_async_copy(received, received, rsem.at[step]).wait

    b_here = exchange(0, lambda m2, q2: s1b.at[m2 * 8 + q2], r1b.at[q, m], r1b)
    a_here = exchange(1, lambda m2, q2: s1a.at[m2 * 8 + q2], r1a.at[q, m], r1a)

    for s in range(8):
        lanes = pl.ds(s * 128, 128)
        gate[:, lanes] = jax.nn.sigmoid(dot(wg_t, zbt[:, lanes]))
        cs = jnp.concatenate([cot[s], cot[8 + s]], axis=0).astype(F32)
        cott[:, lanes] = jnp.transpose(cs)

    def assemble(received, target):
        for p in range(4):
            lanes = pl.ds(p * 128, 128)
            even, odd = pair_up(
                received[2 * p].astype(F32).reshape(128, 128),
                received[2 * p + 1].astype(F32).reshape(128, 128),
            )
            target[:, 0:8, lanes] = even.reshape(16, 8, 128)
            target[:, 8:16, lanes] = odd.reshape(16, 8, 128)

    def to_sibling(n, src, dst):
        copy = pltpu.make_async_remote_copy(
            src_ref=src,
            dst_ref=dst,
            send_sem=sibsem.at[2 * n],
            recv_sem=sibsem.at[2 * n + 1],
            device_id=sibling,
            device_id_type=MESH,
        )
        copy.start()
        return copy.wait

    b_here()
    assemble(r1b, mid)
    bmat[:, pl.ds(h, 1)] = mid[...].astype(BF16).reshape(16, 1, 16, TOKENS)
    b_whole = to_sibling(0, bmat.at[:, h], bmat.at[:, h])
    a_here()
    assemble(r1a, half)
    amat[...] = half[...].reshape(256, TOKENS).astype(BF16)
    b_whole()

    def split(value, p):
        first, second = pair_up(
            value[:, 0:8, :].reshape(128, 128), value[:, 8:16, :].reshape(128, 128)
        )
        return first.reshape(16, 8, 128), second.reshape(16, 8, 128)

    ball = bmat[...].reshape(TOKENS, TOKENS)
    xs = dot(amat[...], ball, 1, 1)
    for p in range(4):
        block = xs[:, p * 128 : (p + 1) * 128].reshape(16, 16, 128)
        first, second = split(block, p)
        s2[2 * p] = first.astype(BF16)
        s2[2 * p + 1] = second.astype(BF16)
    x_here = exchange(2, lambda m2, q2: s2.at[q2, m2], r2.at[me], r2)
    x_here()

    big_a[...] = r2[...].astype(F32).reshape(1024, 128)
    wo_t = jnp.transpose(wo[...].astype(F32)).astype(BF16)
    for s in range(8):
        lanes = pl.ds(s * 128, 128)
        xsl = big_a[pl.ds(s, CH, stride=8), :]
        mean = jnp.mean(xsl, axis=0, keepdims=True)
        centred = xsl - mean
        inv = lax.rsqrt(jnp.mean(centred * centred, axis=0, keepdims=True) + 1e-05)
        xhat = centred * inv
        xb = (xhat * gain2c[...] + bias2c[...]).astype(BF16)
        outp = dot(wo_t, xb)
        g = gate[:, lanes]
        c = cott[:, lanes]
        up_cells = jnp.transpose(g * outp).astype(BF16)
        update[s] = up_cells[0:64]
        update[8 + s] = up_cells[64:128]
        e = (c * g).astype(BF16)
        dgp[:, lanes] = (c * outp * g * (1.0 - g)).astype(BF16)
        dxh = dot(wo[...], e) * gain2c[...]
        dx = inv * (
            dxh
            - jnp.mean(dxh, axis=0, keepdims=True)
            - xhat * jnp.mean(dxh * xhat, axis=0, keepdims=True)
        )
        big_b[pl.ds(s, CH, stride=8), :] = dx
    s3[...] = big_b[...].reshape(CH, 8, 128).astype(BF16)
    dx_here = exchange(3, lambda m2, q2: s3.at[m2 * 8 + q2], r3.at[q, m], r3)
    update_away = pltpu.make_async_copy(update, update_out, outsem.at[0])
    update_away.start()
    pending.append(update_away.wait)
    dx_here()

    assemble(r3, half)
    dxm = half[...].reshape(256, TOKENS)
    da = dot(dxm.astype(BF16), bmat[...].reshape(TOKENS, TOKENS)).reshape(16, 16, TOKENS)
    for p in range(4):
        first, second = split(da[:, :, p * 128 : (p + 1) * 128], p)
        s4a[2 * p] = first.astype(BF16)
        s4a[2 * p + 1] = second.astype(BF16)
    da_here = exchange(4, lambda m2, q2: s4a.at[q2, m2], r4a.at[me], r4a)
    dxm_t = jnp.transpose(dxm).astype(BF16)
    dbs[...] = dot(dxm_t, amat[...]).reshape(16, 2, 16, TOKENS)
    dbsend[...] = dbs[:, pl.ds(1 - h, 1)].reshape(16, 16, TOKENS).astype(BF16)
    db_whole = to_sibling(1, dbsend, dbrecv)
    db_whole()
    mid[...] = dbs[:, pl.ds(h, 1)].reshape(16, 16, TOKENS) + dbrecv[...].astype(F32)
    for p in range(4):
        first, second = split(mid[:, :, pl.ds(p * 128, 128)], p)
        s4b[2 * p] = first.astype(BF16)
        s4b[2 * p + 1] = second.astype(BF16)
    db_here = exchange(5, lambda m2, q2: s4b.at[q2, m2], r4b.at[me], r4b)

    def through_gate(received, big, sig_ref, val_ref, first):
        big[...] = received[...].astype(F32).reshape(1024, 128)
        for s in range(8):
            lanes = pl.ds(s * 128, 128)
            d = big[pl.ds(s, CH, stride=8), :]
            sig = sig_ref[:, lanes]
            dproj[first : first + 128, lanes] = (
                d * val_ref[:, lanes] * sig * (1.0 - sig)
            ).astype(BF16)
            dproj[first + 128 : first + 256, lanes] = (d * sig).astype(BF16)

    da_here()
    through_gate(r4a, big_a, sa, va, 0)
    db_here()
    through_gate(r4b, big_b, sb, vb, 256)

    dw = dot(zbt[...], dproj[...], 1, 1) * (1.0 / TOKENS)
    v = vmat[...]
    nrm = jnp.sqrt(jnp.sum(v * v, axis=0, keepdims=True) + 1e-06)
    scale = mag[...] / nrm
    p_sum = jnp.sum(dw * v, axis=0, keepdims=True)
    dv = dw * scale - v * (mag[...] * p_sum / (nrm * nrm * nrm))
    gd = dot(up[...], dv, 1, 1, precision=HIGHEST)
    gu = dot(down_t[...], dv, precision=HIGHEST)
    gm = p_sum / nrm
    parts[0] = gd[0:8]
    parts[1] = gd[8:16]
    for p in range(4):
        parts[2 + 2 * p] = gu[0:8, p * 128 : (p + 1) * 128]
        parts[3 + 2 * p] = gu[8:16, p * 128 : (p + 1) * 128]
        parts[10, p : p + 1] = gm[:, p * 128 : (p + 1) * 128]
    parts[10, 4:8] = jnp.zeros((4, 128), F32)
    parts[11:16] = jnp.zeros((5, 8, 128), F32)

    f_me = y * 4 + x
    g_me = z * 2 + h

    def in_plane(offset):
        y2 = lax.rem(y + offset[0], NY)
        x2 = lax.rem(x + offset[1], NX)
        device = (4 * z + 2 * lax.rem(y2, 2) + h, x2 * 2 + lax.div(y2, 2))
        return device, y2 * 4 + x2

    def in_column(offset):
        z2 = lax.rem(z + offset[0], NZ)
        h2 = 1 - h if offset[1] else h
        return (4 * z2 + 2 * lax.rem(y, 2) + h2, q), z2 * 2 + h2

    def spread(step, offsets, where, src, own, dst, received):
        pltpu.make_async_copy(src(own), dst, redsem.at[step, 1]).start()
        for offset in offsets:
            if offset == (0, 0):
                continue
            device, other = where(offset)
            pltpu.make_async_remote_copy(
                src_ref=src(other),
                dst_ref=dst,
                send_sem=redsem.at[step, 0],
                recv_sem=redsem.at[step, 1],
                device_id=device,
                device_id_type=MESH,
            ).start()
        others = parts.at[0:15]
        pending.append(pltpu.make_async_copy(others, others, redsem.at[step, 0]).wait)
        return pltpu.make_async_copy(received, received, redsem.at[step, 1]).wait

    plane_here = spread(
        0, FAR_PLANE, in_plane, lambda f: parts.at[f], f_me, level1.at[f_me], level1
    )

    def pair_gradient(s):
        lanes = pl.ds(s * 128, 128)
        dzb = dot(wmat[...], dproj[:, lanes]) + dot(wg[...], dgp[:, lanes])
        dzh = dzb * gain1c[...]
        zh = zhat1[:, lanes]
        dz = inv1[:, lanes] * (
            dzh
            - jnp.mean(dzh, axis=0, keepdims=True)
            - zh * jnp.mean(dzh * zh, axis=0, keepdims=True)
        )
        cells = jnp.transpose(dz).astype(BF16)
        pig[s] = cells[0:64]
        pig[8 + s] = cells[64:128]

    for s in range(0, 3):
        pair_gradient(s)
    plane_here()
    level1[0] = jnp.sum(level1[...], axis=0)
    column_here = spread(
        1, FAR_COLUMN, in_column, lambda g: level1.at[0], g_me, level2.at[g_me], level2
    )
    for s in range(3, 8):
        pair_gradient(s)
    pig_away = pltpu.make_async_copy(pig, pig_out, outsem.at[1])
    pig_away.start()
    pending.append(pig_away.wait)
    column_here()
    level2[0] = jnp.sum(level2[...], axis=0)
    whole_here = spread(
        2, FAR_PLANE, in_plane, lambda f: level2.at[0], f_me, whole.at[f_me], whole
    )
    whole_here()
    finish()


def unpack(update_in, pig_in, whole_in, update, pig, gdown, gup, gmag, *scratch):
    here, (insem, outsem) = scratch[:3], scratch[3:]
    loads = [
        pltpu.make_async_copy(src, dst, insem.at[n])
        for n, (src, dst) in enumerate(zip((update_in, pig_in, whole_in), here))
    ]
    for load in loads:
        load.start()
    stores = []
    for n, dst in enumerate((update, pig)):
        loads[n].wait()
        stores.append(pltpu.make_async_copy(here[n], dst, outsem.at[n]))
        stores[n].start()
    loads[2].wait()
    whole = here[2]
    gdown[...] = whole[0:2].reshape(16, 128)
    for p in range(4):
        gup[:, p * 128 : (p + 1) * 128] = whole[2 + 2 * p : 4 + 2 * p].reshape(16, 128)
        gmag[:, p * 128 : (p + 1) * 128] = whole[10, p : p + 1]
    for store in stores:
        store.wait()


def on_device(
    pair,
    input_norm_gain,
    input_norm_bias,
    frozen_base_weight,
    adapter_down_factor,
    adapter_up_factor,
    magnitude,
    output_gate_weight,
    output_projection_weight,
    centre_norm_gain,
    centre_norm_bias,
    cotangent,
):
    vmem = pl.BlockSpec(memory_space=pltpu.VMEM)
    hbm = pl.BlockSpec(memory_space=pltpu.HBM)
    cells = (CH, 1024)
    message = (CH, 8, 128)
    by_chip = (8, 16, 8, 128)
    operands = (
        pair,
        input_norm_gain.reshape(1, CH),
        input_norm_bias.reshape(1, CH),
        frozen_base_weight,
        adapter_down_factor.T,
        adapter_up_factor,
        magnitude.reshape(1, 4 * CH),
        output_gate_weight,
        output_projection_weight,
        centre_norm_gain.reshape(1, CH),
        centre_norm_bias.reshape(1, CH),
        cotangent,
    )
    block = jax.ShapeDtypeStruct(pair.shape, BF16)
    update, pig, whole = pl.pallas_call(
        kernel,
        out_shape=(block, block, jax.ShapeDtypeStruct((16, 8, 128), F32)),
        in_specs=[hbm] * 12,
        out_specs=(hbm, hbm, vmem),
        scratch_shapes=[pltpu.VMEM(a.shape, a.dtype) for a in operands]
        + [
            pltpu.VMEM(pair.shape, BF16),
            pltpu.VMEM(pair.shape, BF16),
            pltpu.VMEM(message, BF16),
            pltpu.VMEM(message, BF16),
            pltpu.VMEM(by_chip, BF16),
            pltpu.VMEM(by_chip, BF16),
            pltpu.VMEM(by_chip, BF16),
            pltpu.VMEM(message, BF16),
            pltpu.VMEM(message, BF16),
            pltpu.VMEM(by_chip, BF16),
            pltpu.VMEM(by_chip, BF16),
            pltpu.VMEM(by_chip, BF16),
            pltpu.VMEM(message, BF16),
            pltpu.VMEM(message, BF16),
            pltpu.VMEM((256, TOKENS), BF16),
            pltpu.VMEM((16, 2, 16, TOKENS), BF16),
            pltpu.VMEM((16, 16, TOKENS), BF16),
            pltpu.VMEM((16, 16, TOKENS), BF16),
            pltpu.VMEM((1024, 128), F32),
            pltpu.VMEM((1024, 128), F32),
            pltpu.VMEM((16, 16, TOKENS), F32),
            pltpu.VMEM((16, 16, TOKENS), F32),
            pltpu.VMEM((16, 2, 16, TOKENS), F32),
            pltpu.VMEM(cells, F32),
            pltpu.VMEM(cells, F32),
            pltpu.VMEM(cells, F32),
            pltpu.VMEM(cells, F32),
            pltpu.VMEM(cells, F32),
            pltpu.VMEM((1, 1024), F32),
            pltpu.VMEM(cells, BF16),
            pltpu.VMEM(cells, F32),
            pltpu.VMEM(cells, F32),
            pltpu.VMEM(cells, BF16),
            pltpu.VMEM((4 * CH, 1024), BF16),
            pltpu.VMEM((CH, 4 * CH), F32),
            pltpu.VMEM((CH, 4 * CH), BF16),
            pltpu.VMEM((4 * CH, CH), BF16),
            pltpu.VMEM((CH, 128), F32),
            pltpu.VMEM((CH, 128), F32),
            pltpu.VMEM((CH, 128), F32),
            pltpu.VMEM((16, 8, 128), F32),
            pltpu.VMEM((16, 8, 128), F32),
            pltpu.VMEM((16, 8, 128), F32),
            pltpu.SemaphoreType.DMA((6,)),
            pltpu.SemaphoreType.DMA((6,)),
            pltpu.SemaphoreType.DMA((4,)),
            pltpu.SemaphoreType.DMA((3, 2)),
            pltpu.SemaphoreType.DMA((12,)),
            pltpu.SemaphoreType.DMA((2,)),
        ],
        compiler_params=pltpu.CompilerParams(
            collective_id=0, has_side_effects=True, vmem_limit_bytes=VMEM_GRANT
        ),
    )(*operands)
    update, pig, gdown, gup, gmag = pl.pallas_call(
        unpack,
        out_shape=(
            block,
            block,
            jax.ShapeDtypeStruct((16, CH), F32),
            jax.ShapeDtypeStruct((16, 4 * CH), F32),
            jax.ShapeDtypeStruct((1, 4 * CH), F32),
        ),
        in_specs=[hbm] * 3,
        out_specs=(hbm, hbm, vmem, vmem, vmem),
        scratch_shapes=[
            pltpu.VMEM(block.shape, BF16),
            pltpu.VMEM(block.shape, BF16),
            pltpu.VMEM((16, 8, 128), F32),
            pltpu.SemaphoreType.DMA((3,)),
            pltpu.SemaphoreType.DMA((2,)),
        ],
        compiler_params=pltpu.CompilerParams(vmem_limit_bytes=VMEM_GRANT),
    )(update, pig, whole)
    return update, pig, gdown.T, gup, gmag.reshape(4 * CH)


def solution(mesh):
    cells = P("row", "col", None)
    placed = (cells,) + (P(),) * 10 + (cells,)
    return jax.shard_map(
        on_device,
        mesh=mesh,
        in_specs=placed,
        out_specs=(cells, cells, P(), P(), P()),
        check_vma=False,
    )
```

time: 97.7 us -> 78.2 us (0.80)
  Pallas kernels: 88.3 us -> 77.4 us
  local copies, waits for them, and re-layouts: 8.31 us -> 0 us
    pallas_call x1 -> x2, Pallas kernels: 88.3 us -> 77.4 us  [the longest x1 75 us: on_device(): pl.pallas_call(kernel, out_shape=(block, block, jax.ShapeDtypeStruct((16,...]
    unnamed x30 -> x0, local copies, waits for them, and re-layouts: 8.31 us -> none
where the time goes in v2:
time: 78.2 us; the launch traced here: 78.1 us
  Pallas kernels  77.4 us (99%)
    pallas_call x1, Pallas kernels, on_device(): pl.pallas_call(kernel, out_shape=(block, block, jax.ShapeDtypeStruct((16,...  75 us
    pallas_call x1, Pallas kernels, on_device(): pl.pallas_call(unpack, out_shape=(block, block, jax.ShapeDtypeStruct((16,...  2.4 us

profile of v2, /device:TPU:1, one launch (start us, length us, event | category | flops | bytes accessed | tf_op | source)
XLA Modules:
  0.0 78.1 jit_solution(11515542599839513247)
XLA Ops:
  0.6 75.0 %shard_map.155 = (bf16[16,64,128]{2,1,0:T(8,128)(2,1)}, bf16[16,64,128]{2,1,0:T(8,128)(2,1)}, f32[16,8,128]{2,1,0:T(8,128)}) custom-call(bf16[16,64,128]{2,1,0:T(8,128)(2,1)} %refs_0_.1, f32[1,128]{1,0:T(1,128)} %bitcast.10, f32[1,128]{1,0:T(1,128)} %bitcast.11, f32[128,512]{1,0:T(8,128)} %refs_3_.1, f32[16,128]{1,0:T(8,128)} %bitcast.8, f32[16,512]{1,0:T(8,128)} %refs_5_.1, ...), custom_call_target="tpu_custom_call" | custom-call | tf_op jit(solution)/shard_map/pallas_call | solution.py:506
  75.7 2.4 %shard_map.156 = (bf16[16,64,128]{2,1,0:T(8,128)(2,1)}, bf16[16,64,128]{2,1,0:T(8,128)(2,1)}, f32[16,128]{1,0:T(8,128)}, f32[16,512]{1,0:T(8,128)}, f32[1,512]{1,0:T(1,128)}) custom-call(bf16[16,64,128]{2,1,0:T(8,128)(2,1)} %get-tuple-element.13.update_in, bf16[16,64,128]{2,1,0:T(8,128)(2,1)} %get-tuple-element.14.pig_in, ...), custom_call_target="tpu_custom_call" | custom-call | tf_op jit(solution)/shard_map/pallas_call | solution.py:567

commit v3 on v2

--- a/solution.py
+++ b/solution.py
@@ -34,16 +34,17 @@
     return n // 2 + (1 - 2 * lax.rem(k, 2)) * lax.div(k + 1, 2)
 
 
-def low_half(shape):
-    return lax.broadcasted_iota(jnp.int32, shape, 1) < 64
-
-
 def pair_up(first, second):
-    low = low_half(first.shape)
+    last = first.ndim - 1
+    low = lax.broadcasted_iota(jnp.int32, first.shape, last) < 64
     return (
-        jnp.where(low, first, pltpu.roll(second, 64, 1)),
-        jnp.where(low, pltpu.roll(first, 64, 1), second),
+        jnp.where(low, first, pltpu.roll(second, 64, last)),
+        jnp.where(low, pltpu.roll(first, 64, last), second),
     )
+
+
+def half_rows(big, u):
+    return big[...].reshape(CH, 8, 128)[:, 4 * u : 4 * u + 4, :].astype(BF16)
 
 
 def column(row_ref):
@@ -152,21 +153,22 @@
         for z_row in z_rows[:-1]:
             act(z_row + parity, q2)
 
-    barrier = pltpu.get_barrier_semaphore()
-
-    def greet(row2, q2):
-        pl.semaphore_signal(barrier, inc=1, device_id=(row2, q2), device_id_type=MESH)
-
-    to_all(greet)
-    for z_row in z_rows:
-        greet(z_row + 2 * lax.rem(y, 2) + 1 - 2 * h, q)
-
     loads = [
         pltpu.make_async_copy(operand, here, insem.at[n])
         for n, (operand, here) in enumerate(zip(operands, local))
     ]
     for load in loads:
         load.start()
+
+    barrier = pltpu.get_barrier_semaphore()
+
+    def greet(row2, q2):
+        pl.semaphore_signal(barrier, inc=1, device_id=(row2, q2), device_id_type=MESH)
+
+    to_all(greet)
+    for z_row in z_rows:
+        greet(z_row + 2 * lax.rem(y, 2) + 1 - 2 * h, q)
+
     for load in loads:
         load.wait()
     pending = []
@@ -188,6 +190,14 @@
     gain2c[...] = column(gain2)
     bias2c[...] = column(bias2)
 
+    def project(s, zb, first, sig_ref, val_ref, big):
+        lanes = pl.ds(s * 128, 128)
+        proj = dot(wmat_t[first : first + 256], zb)
+        sig = jax.nn.sigmoid(proj[0:128])
+        sig_ref[:, lanes] = sig
+        val_ref[:, lanes] = proj[128:256]
+        big[pl.ds(s, CH, stride=8), :] = sig * proj[128:256]
+
     for s in range(8):
         lanes = pl.ds(s * 128, 128)
         zs = jnp.concatenate([pair[s], pair[8 + s]], axis=0).astype(F32)
@@ -200,21 +210,12 @@
         inv1[:, lanes] = inv
         zb = (zh * gain1c[...] + bias1c).astype(BF16)
         zbt[:, lanes] = zb
-        proj = dot(wmat_t[...], zb)
-        sig_a = jax.nn.sigmoid(proj[0:128])
-        sig_b = jax.nn.sigmoid(proj[256:384])
-        sa[:, lanes] = sig_a
-        va[:, lanes] = proj[128:256]
-        sb[:, lanes] = sig_b
-        vb[:, lanes] = proj[384:512]
-        big_a[pl.ds(s, CH, stride=8), :] = sig_a * proj[128:256]
-        big_b[pl.ds(s, CH, stride=8), :] = sig_b * proj[384:512]
+        project(s, zb, 256, sb, vb, big_b)
     s1b[...] = big_b[...].reshape(CH, 8, 128).astype(BF16)
-    s1a[...] = big_a[...].reshape(CH, 8, 128).astype(BF16)
 
     pl.semaphore_wait(barrier, 127 + NZ)
 
-    def exchange(step, src, dst_slot, received):
+    def exchange(step, src, dst_slot, received, others):
         own = pltpu.make_async_copy(src(m, q), dst_slot, rsem.at[step])
         own.start()
 
@@ -229,12 +230,34 @@
             ).start()
 
         to_all(send)
-        others = s1a.at[0:127]
         pending.append(pltpu.make_async_copy(others, others, ssem.at[step]).wait)
         return pltpu.make_async_copy(received, received, rsem.at[step]).wait
 
-    b_here = exchange(0, lambda m2, q2: s1b.at[m2 * 8 + q2], r1b.at[q, m], r1b)
-    a_here = exchange(1, lambda m2, q2: s1a.at[m2 * 8 + q2], r1a.at[q, m], r1a)
+    def from_cells(step, sent, received):
+        return exchange(
+            step,
+            lambda m2, q2: sent.at[m2 * 8 + q2],
+            received.at[q, m],
+            received,
+            sent.at[0:127],
+        )
+
+    def from_owner(step, sent, received):
+        return exchange(
+            step,
+            lambda m2, q2: sent.at[q2, m2],
+            received.at[me],
+            received,
+            received.at[0:127],
+        )
+
+    b_here = from_cells(0, s1b, r1b)
+    a_here = []
+    for u in range(2):
+        for s in range(4 * u, 4 * u + 4):
+            project(s, zbt[:, pl.ds(s * 128, 128)], 0, sa, va, big_a)
+        s1a[u] = half_rows(big_a, u)
+        a_here.append(from_cells(1 + u, s1a.at[u], r1a.at[u]))
 
     for s in range(8):
         lanes = pl.ds(s * 128, 128)
@@ -243,14 +266,20 @@
         cott[:, lanes] = jnp.transpose(cs)
 
     def assemble(received, target):
+        rows = received.shape[2]
         for p in range(4):
             lanes = pl.ds(p * 128, 128)
-            even, odd = pair_up(
-                received[2 * p].astype(F32).reshape(128, 128),
-                received[2 * p + 1].astype(F32).reshape(128, 128),
-            )
-            target[:, 0:8, lanes] = even.reshape(16, 8, 128)
-            target[:, 8:16, lanes] = odd.reshape(16, 8, 128)
+            even, odd = pair_up(received[2 * p].astype(F32), received[2 * p + 1].astype(F32))
+            target[:, 0:rows, lanes] = even
+            target[:, rows : 2 * rows, lanes] = odd
+
+    def dispatch(value, messages):
+        rows = value.shape[1] // 2
+        for p in range(4):
+            block = value[:, :, p * 128 : (p + 1) * 128]
+            first, second = pair_up(block[:, 0:rows, :], block[:, rows : 2 * rows, :])
+            messages[2 * p] = first.astype(BF16)
+            messages[2 * p + 1] = second.astype(BF16)
 
     def to_sibling(n, src, dst):
         copy = pltpu.make_async_remote_copy(
@@ -268,30 +297,20 @@
     assemble(r1b, mid)
     bmat[:, pl.ds(h, 1)] = mid[...].astype(BF16).reshape(16, 1, 16, TOKENS)
     b_whole = to_sibling(0, bmat.at[:, h], bmat.at[:, h])
-    a_here()
-    assemble(r1a, half)
-    amat[...] = half[...].reshape(256, TOKENS).astype(BF16)
-    b_whole()
-
-    def split(value, p):
-        first, second = pair_up(
-            value[:, 0:8, :].reshape(128, 128), value[:, 8:16, :].reshape(128, 128)
-        )
-        return first.reshape(16, 8, 128), second.reshape(16, 8, 128)
-
-    ball = bmat[...].reshape(TOKENS, TOKENS)
-    xs = dot(amat[...], ball, 1, 1)
-    for p in range(4):
-        block = xs[:, p * 128 : (p + 1) * 128].reshape(16, 16, 128)
-        first, second = split(block, p)
-        s2[2 * p] = first.astype(BF16)
-        s2[2 * p + 1] = second.astype(BF16)
-    x_here = exchange(2, lambda m2, q2: s2.at[q2, m2], r2.at[me], r2)
-    x_here()
-
-    big_a[...] = r2[...].astype(F32).reshape(1024, 128)
+    x_here = []
+    for u in range(2):
+        a_here[u]()
+        assemble(r1a.at[u], half)
+        amat[u] = half[...].reshape(128, TOKENS).astype(BF16)
+        if u == 0:
+            b_whole()
+        ball = bmat[...].reshape(TOKENS, TOKENS)
+        dispatch(dot(amat[u], ball, 1, 1).reshape(16, 8, TOKENS), s2.at[u])
+        x_here.append(from_owner(3 + u, s2.at[u], r2.at[u]))
+
     wo_t = jnp.transpose(wo[...].astype(F32)).astype(BF16)
-    for s in range(8):
+
+    def centre(s):
         lanes = pl.ds(s * 128, 128)
         xsl = big_a[pl.ds(s, CH, stride=8), :]
         mean = jnp.mean(xsl, axis=0, keepdims=True)
@@ -314,66 +333,83 @@
             - xhat * jnp.mean(dxh * xhat, axis=0, keepdims=True)
         )
         big_b[pl.ds(s, CH, stride=8), :] = dx
-    s3[...] = big_b[...].reshape(CH, 8, 128).astype(BF16)
-    dx_here = exchange(3, lambda m2, q2: s3.at[m2 * 8 + q2], r3.at[q, m], r3)
+
+    def received_half(received, big, u):
+        big.reshape(CH, 8, 128)[:, 4 * u : 4 * u + 4, :] = received[...].astype(F32)
+
+    dx_here = []
+    for u in range(2):
+        x_here[u]()
+        received_half(r2.at[u], big_a, u)
+        for s in range(4 * u, 4 * u + 4):
+            centre(s)
+        s3[u] = half_rows(big_b, u)
+        dx_here.append(from_cells(5 + u, s3.at[u], r3.at[u]))
     update_away = pltpu.make_async_copy(update, update_out, outsem.at[0])
     update_away.start()
     pending.append(update_away.wait)
-    dx_here()
-
-    assemble(r3, half)
-    dxm = half[...].reshape(256, TOKENS)
-    da = dot(dxm.astype(BF16), bmat[...].reshape(TOKENS, TOKENS)).reshape(16, 16, TOKENS)
-    for p in range(4):
-        first, second = split(da[:, :, p * 128 : (p + 1) * 128], p)
-        s4a[2 * p] = first.astype(BF16)
-        s4a[2 * p + 1] = second.astype(BF16)
-    da_here = exchange(4, lambda m2, q2: s4a.at[q2, m2], r4a.at[me], r4a)
-    dxm_t = jnp.transpose(dxm).astype(BF16)
-    dbs[...] = dot(dxm_t, amat[...]).reshape(16, 2, 16, TOKENS)
-    dbsend[...] = dbs[:, pl.ds(1 - h, 1)].reshape(16, 16, TOKENS).astype(BF16)
-    db_whole = to_sibling(1, dbsend, dbrecv)
+
+    da_here = []
+    for u in range(2):
+        dx_here[u]()
+        assemble(r3.at[u], half)
+        dxm = half[...].reshape(128, TOKENS)
+        db_part = dot(jnp.transpose(dxm).astype(BF16), amat[u]).reshape(16, 2, 16, TOKENS)
+        if u == 0:
+            dbs[...] = db_part
+        else:
+            dbs[...] += db_part
+            dbsend[...] = dbs[:, pl.ds(1 - h, 1)].reshape(16, 16, TOKENS).astype(BF16)
+            db_whole = to_sibling(1, dbsend, dbrecv)
+        da = dot(dxm.astype(BF16), bmat[...].reshape(TOKENS, TOKENS))
+        dispatch(da.reshape(16, 8, TOKENS), s4a.at[u])
+        da_here.append(from_owner(7 + u, s4a.at[u], r4a.at[u]))
     db_whole()
     mid[...] = dbs[:, pl.ds(h, 1)].reshape(16, 16, TOKENS) + dbrecv[...].astype(F32)
-    for p in range(4):
-        first, second = split(mid[:, :, pl.ds(p * 128, 128)], p)
-        s4b[2 * p] = first.astype(BF16)
-        s4b[2 * p + 1] = second.astype(BF16)
-    db_here = exchange(5, lambda m2, q2: s4b.at[q2, m2], r4b.at[me], r4b)
-
-    def through_gate(received, big, sig_ref, val_ref, first):
-        big[...] = received[...].astype(F32).reshape(1024, 128)
-        for s in range(8):
-            lanes = pl.ds(s * 128, 128)
-            d = big[pl.ds(s, CH, stride=8), :]
-            sig = sig_ref[:, lanes]
-            dproj[first : first + 128, lanes] = (
-                d * val_ref[:, lanes] * sig * (1.0 - sig)
-            ).astype(BF16)
-            dproj[first + 128 : first + 256, lanes] = (d * sig).astype(BF16)
-
-    da_here()
-    through_gate(r4a, big_a, sa, va, 0)
+    dispatch(mid[...], s4b)
+    db_here = from_owner(9, s4b, r4b)
+
+    def through_gate(s, big, sig_ref, val_ref, first):
+        lanes = pl.ds(s * 128, 128)
+        d = big[pl.ds(s, CH, stride=8), :]
+        sig = sig_ref[:, lanes]
+        dproj[first : first + 128, lanes] = (
+            d * val_ref[:, lanes] * sig * (1.0 - sig)
+        ).astype(BF16)
+        dproj[first + 128 : first + 256, lanes] = (d * sig).astype(BF16)
+
+    def weight_part(n):
+        half_of = slice(n * 256, n * 256 + 256)
+        dw = dot(zbt[...], dproj[half_of, :], 1, 1) * (1.0 / TOKENS)
+        v = vmat[:, half_of]
+        mg = mag[:, half_of]
+        nrm = jnp.sqrt(jnp.sum(v * v, axis=0, keepdims=True) + 1e-06)
+        p_sum = jnp.sum(dw * v, axis=0, keepdims=True)
+        dv = dw * (mg / nrm) - v * (mg * p_sum / (nrm * nrm * nrm))
+        gu = dot(down_t[...], dv, precision=HIGHEST)
+        gm = p_sum / nrm
+        for p in range(2):
+            lanes = slice(p * 128, p * 128 + 128)
+            parts[2 + 4 * n + 2 * p] = gu[0:8, lanes]
+            parts[3 + 4 * n + 2 * p] = gu[8:16, lanes]
+            parts[10, 2 * n + p : 2 * n + p + 1] = gm[:, lanes]
+        return dot(up[:, half_of], dv, 1, 1, precision=HIGHEST)
+
+    parts[10, 4:8] = jnp.zeros((4, 128), F32)
+    parts[11:16] = jnp.zeros((5, 8, 128), F32)
+    for u in range(2):
+        da_here[u]()
+        received_half(r4a.at[u], big_a, u)
+        for s in range(4 * u, 4 * u + 4):
+            through_gate(s, big_a, sa, va, 0)
+    gd = weight_part(0)
     db_here()
-    through_gate(r4b, big_b, sb, vb, 256)
-
-    dw = dot(zbt[...], dproj[...], 1, 1) * (1.0 / TOKENS)
-    v = vmat[...]
-    nrm = jnp.sqrt(jnp.sum(v * v, axis=0, keepdims=True) + 1e-06)
-    scale = mag[...] / nrm
-    p_sum = jnp.sum(dw * v, axis=0, keepdims=True)
-    dv = dw * scale - v * (mag[...] * p_sum / (nrm * nrm * nrm))
-    gd = dot(up[...], dv, 1, 1, precision=HIGHEST)
-    gu = dot(down_t[...], dv, precision=HIGHEST)
-    gm = p_sum / nrm
+    big_b[...] = r4b[...].astype(F32).reshape(1024, 128)
+    for s in range(8):
+        through_gate(s, big_b, sb, vb, 256)
+    gd = gd + weight_part(1)
     parts[0] = gd[0:8]
     parts[1] = gd[8:16]
-    for p in range(4):
-        parts[2 + 2 * p] = gu[0:8, p * 128 : (p + 1) * 128]
-        parts[3 + 2 * p] = gu[8:16, p * 128 : (p + 1) * 128]
-        parts[10, p : p + 1] = gm[:, p * 128 : (p + 1) * 128]
-    parts[10, 4:8] = jnp.zeros((4, 128), F32)
-    parts[11:16] = jnp.zeros((5, 8, 128), F32)
 
     f_me = y * 4 + x
     g_me = z * 2 + h
@@ -446,27 +482,35 @@
     finish()
 
 
-def unpack(update_in, pig_in, whole_in, update, pig, gdown, gup, gmag, *scratch):
-    here, (insem, outsem) = scratch[:3], scratch[3:]
+def unpack(whole_in, update_in, pig_in, gdown, gup, gmag, update, pig, *scratch):
+    (whole, update_here, pig_here, gup_here, gmag_here, insem, outsem) = scratch
+    here = (whole, update_here, pig_here)
     loads = [
         pltpu.make_async_copy(src, dst, insem.at[n])
-        for n, (src, dst) in enumerate(zip((update_in, pig_in, whole_in), here))
+        for n, (src, dst) in enumerate(zip((whole_in, update_in, pig_in), here))
     ]
     for load in loads:
         load.start()
     stores = []
-    for n, dst in enumerate((update, pig)):
-        loads[n].wait()
-        stores.append(pltpu.make_async_copy(here[n], dst, outsem.at[n]))
-        stores[n].start()
+
+    def store(src, dst):
+        stores.append(pltpu.make_async_copy(src, dst, outsem.at[len(stores)]))
+        stores[-1].start()
+
+    loads[0].wait()
+    for n in range(2):
+        store(whole.at[n], gdown.at[pl.ds(8 * n, 8)])
+    for p in range(4):
+        gup_here[:, p * 128 : (p + 1) * 128] = whole[2 + 2 * p : 4 + 2 * p].reshape(16, 128)
+        gmag_here[:, p * 128 : (p + 1) * 128] = whole[10, p : p + 1]
+    store(gup_here, gup)
+    store(gmag_here, gmag)
+    loads[1].wait()
+    store(update_here, update)
     loads[2].wait()
-    whole = here[2]
-    gdown[...] = whole[0:2].reshape(16, 128)
-    for p in range(4):
-        gup[:, p * 128 : (p + 1) * 128] = whole[2 + 2 * p : 4 + 2 * p].reshape(16, 128)
-        gmag[:, p * 128 : (p + 1) * 128] = whole[10, p : p + 1]
-    for store in stores:
-        store.wait()
+    store(pig_here, pig)
+    for copy in stores:
+        copy.wait()
 
 
 def on_device(
@@ -483,11 +527,12 @@
     centre_norm_bias,
     cotangent,
 ):
-    vmem = pl.BlockSpec(memory_space=pltpu.VMEM)
     hbm = pl.BlockSpec(memory_space=pltpu.HBM)
     cells = (CH, 1024)
     message = (CH, 8, 128)
     by_chip = (8, 16, 8, 128)
+    message_halves = (2, CH, 4, 128)
+    by_chip_halves = (2, 8, 16, 4, 128)
     operands = (
         pair,
         input_norm_gain.reshape(1, CH),
@@ -507,31 +552,31 @@
         kernel,
         out_shape=(block, block, jax.ShapeDtypeStruct((16, 8, 128), F32)),
         in_specs=[hbm] * 12,
-        out_specs=(hbm, hbm, vmem),
+        out_specs=(hbm, hbm, hbm),
         scratch_shapes=[pltpu.VMEM(a.shape, a.dtype) for a in operands]
         + [
             pltpu.VMEM(pair.shape, BF16),
             pltpu.VMEM(pair.shape, BF16),
+            pltpu.VMEM(message_halves, BF16),
             pltpu.VMEM(message, BF16),
+            pltpu.VMEM(by_chip_halves, BF16),
+            pltpu.VMEM(by_chip, BF16),
+            pltpu.VMEM(by_chip_halves, BF16),
+            pltpu.VMEM(message_halves, BF16),
+            pltpu.VMEM(message_halves, BF16),
+            pltpu.VMEM(by_chip_halves, BF16),
+            pltpu.VMEM(by_chip_halves, BF16),
+            pltpu.VMEM(by_chip, BF16),
+            pltpu.VMEM(message_halves, BF16),
             pltpu.VMEM(message, BF16),
-            pltpu.VMEM(by_chip, BF16),
-            pltpu.VMEM(by_chip, BF16),
-            pltpu.VMEM(by_chip, BF16),
-            pltpu.VMEM(message, BF16),
-            pltpu.VMEM(message, BF16),
-            pltpu.VMEM(by_chip, BF16),
-            pltpu.VMEM(by_chip, BF16),
-            pltpu.VMEM(by_chip, BF16),
-            pltpu.VMEM(message, BF16),
-            pltpu.VMEM(message, BF16),
-            pltpu.VMEM((256, TOKENS), BF16),
+            pltpu.VMEM((2, 128, TOKENS), BF16),
             pltpu.VMEM((16, 2, 16, TOKENS), BF16),
             pltpu.VMEM((16, 16, TOKENS), BF16),
             pltpu.VMEM((16, 16, TOKENS), BF16),
             pltpu.VMEM((1024, 128), F32),
             pltpu.VMEM((1024, 128), F32),
             pltpu.VMEM((16, 16, TOKENS), F32),
-            pltpu.VMEM((16, 16, TOKENS), F32),
+            pltpu.VMEM((16, 8, TOKENS), F32),
             pltpu.VMEM((16, 2, 16, TOKENS), F32),
             pltpu.VMEM(cells, F32),
             pltpu.VMEM(cells, F32),
@@ -553,8 +598,8 @@
             pltpu.VMEM((16, 8, 128), F32),
             pltpu.VMEM((16, 8, 128), F32),
             pltpu.VMEM((16, 8, 128), F32),
-            pltpu.SemaphoreType.DMA((6,)),
-            pltpu.SemaphoreType.DMA((6,)),
+            pltpu.SemaphoreType.DMA((10,)),
+            pltpu.SemaphoreType.DMA((10,)),
             pltpu.SemaphoreType.DMA((4,)),
             pltpu.SemaphoreType.DMA((3, 2)),
             pltpu.SemaphoreType.DMA((12,)),
@@ -564,26 +609,28 @@
             collective_id=0, has_side_effects=True, vmem_limit_bytes=VMEM_GRANT
         ),
     )(*operands)
-    update, pig, gdown, gup, gmag = pl.pallas_call(
+    gdown, gup, gmag, update, pig = pl.pallas_call(
         unpack,
         out_shape=(
-            block,
-            block,
             jax.ShapeDtypeStruct((16, CH), F32),
             jax.ShapeDtypeStruct((16, 4 * CH), F32),
             jax.ShapeDtypeStruct((1, 4 * CH), F32),
+            block,
+            block,
         ),
         in_specs=[hbm] * 3,
-        out_specs=(hbm, hbm, vmem, vmem, vmem),
+        out_specs=(hbm,) * 5,
         scratch_shapes=[
+            pltpu.VMEM((16, 8, 128), F32),
             pltpu.VMEM(block.shape, BF16),
             pltpu.VMEM(block.shape, BF16),
-            pltpu.VMEM((16, 8, 128), F32),
+            pltpu.VMEM((16, 4 * CH), F32),
+            pltpu.VMEM((1, 4 * CH), F32),
             pltpu.SemaphoreType.DMA((3,)),
-            pltpu.SemaphoreType.DMA((2,)),
+            pltpu.SemaphoreType.DMA((6,)),
         ],
         compiler_params=pltpu.CompilerParams(vmem_limit_bytes=VMEM_GRANT),
-    )(update, pig, whole)
+    )(whole, update, pig)
     return update, pig, gdown.T, gup, gmag.reshape(4 * CH)
 
 

time: 78.2 us -> 76.3 us (0.976)
  Pallas kernels: 77.4 us -> 75.6 us
    pallas_call x1, Pallas kernels: 75 us -> 73.7 us  [on_device(): pl.pallas_call(kernel, out_shape=(block, block, jax.ShapeDtypeStruct((16,...]
where the time goes in v3:
time: 76.3 us; the launch traced here: 76.2 us
  Pallas kernels  75.6 us (99%)
    pallas_call x1, Pallas kernels, on_device(): pl.pallas_call(kernel, out_shape=(block, block, jax.ShapeDtypeStruct((16,...  73.7 us
    pallas_call x1, Pallas kernels, on_device(): pl.pallas_call(unpack, out_shape=(jax.ShapeDtypeStruct((16, CH), F32), ja...  1.86 us

profile of v3, /device:TPU:1, one launch (start us, length us, event | category | flops | bytes accessed | tf_op | source)
XLA Modules:
  0.0 76.2 jit_solution(402994712613769314)
XLA Ops:
  0.6 73.7 %shard_map.155 = (bf16[16,64,128]{2,1,0:T(8,128)(2,1)}, bf16[16,64,128]{2,1,0:T(8,128)(2,1)}, f32[16,8,128]{2,1,0:T(8,128)}) custom-call(bf16[16,64,128]{2,1,0:T(8,128)(2,1)} %refs_0_.1, f32[1,128]{1,0:T(1,128)} %bitcast.10, f32[1,128]{1,0:T(1,128)} %bitcast.11, f32[128,512]{1,0:T(8,128)} %refs_3_.1, f32[16,128]{1,0:T(8,128)} %bitcast.8, f32[16,512]{1,0:T(8,128)} %refs_5_.1, ...), custom_call_target="tpu_custom_call" | custom-call | tf_op jit(solution)/shard_map/pallas_call | solution.py:551
  74.4 1.9 %shard_map.156 = (f32[16,128]{1,0:T(8,128)}, f32[16,512]{1,0:T(8,128)}, f32[1,512]{1,0:T(1,128)}, bf16[16,64,128]{2,1,0:T(8,128)(2,1)}, bf16[16,64,128]{2,1,0:T(8,128)(2,1)}) custom-call(f32[16,8,128]{2,1,0:T(8,128)} %get-tuple-element.13.whole_in, bf16[16,64,128]{2,1,0:T(8,128)(2,1)} %get-tuple-element.14.update_in, ...), custom_call_target="tpu_custom_call" | custom-call | tf_op jit(solution)/shard_map/pallas_call | solution.py:612

commit v4 on v3

--- a/solution.py
+++ b/solution.py
@@ -100,6 +100,8 @@
         gate,
         cott,
         dgp,
+        dxhat,
+        xbt,
         dproj,
         vmat,
         wmat,
@@ -195,8 +197,9 @@
         proj = dot(wmat_t[first : first + 256], zb)
         sig = jax.nn.sigmoid(proj[0:128])
         sig_ref[:, lanes] = sig
-        val_ref[:, lanes] = proj[128:256]
-        big[pl.ds(s, CH, stride=8), :] = sig * proj[128:256]
+        gated = sig * proj[128:256]
+        val_ref[:, lanes] = gated * (1.0 - sig)
+        big[pl.ds(s, CH, stride=8), :] = gated
 
     for s in range(8):
         lanes = pl.ds(s * 128, 128)
@@ -245,7 +248,7 @@
     def from_owner(step, sent, received):
         return exchange(
             step,
-            lambda m2, q2: sent.at[q2, m2],
+            lambda m2, q2: sent.at[m2, q2],
             received.at[me],
             received,
             received.at[0:127],
@@ -261,9 +264,13 @@
 
     for s in range(8):
         lanes = pl.ds(s * 128, 128)
-        gate[:, lanes] = jax.nn.sigmoid(dot(wg_t, zbt[:, lanes]))
+        g = jax.nn.sigmoid(dot(wg_t, zbt[:, lanes]))
+        gate[:, lanes] = g
         cs = jnp.concatenate([cot[s], cot[8 + s]], axis=0).astype(F32)
-        cott[:, lanes] = jnp.transpose(cs)
+        cs = jnp.transpose(cs)
+        cott[:, lanes] = cs
+        dxh = dot(wo[...], (cs * g).astype(BF16)) * gain2c[...]
+        dxhat[:, lanes] = dxh - jnp.mean(dxh, axis=0, keepdims=True)
 
     def assemble(received, target):
         rows = received.shape[2]
@@ -278,8 +285,8 @@
         for p in range(4):
             block = value[:, :, p * 128 : (p + 1) * 128]
             first, second = pair_up(block[:, 0:rows, :], block[:, rows : 2 * rows, :])
-            messages[2 * p] = first.astype(BF16)
-            messages[2 * p + 1] = second.astype(BF16)
+            messages[:, 2 * p] = first.astype(BF16)
+            messages[:, 2 * p + 1] = second.astype(BF16)
 
     def to_sibling(n, src, dst):
         copy = pltpu.make_async_remote_copy(
@@ -317,22 +324,19 @@
         centred = xsl - mean
         inv = lax.rsqrt(jnp.mean(centred * centred, axis=0, keepdims=True) + 1e-05)
         xhat = centred * inv
-        xb = (xhat * gain2c[...] + bias2c[...]).astype(BF16)
-        outp = dot(wo_t, xb)
+        xbt[:, lanes] = (xhat * gain2c[...] + bias2c[...]).astype(BF16)
+        dxh = dxhat[:, lanes]
+        dx = inv * (dxh - xhat * jnp.mean(dxh * xhat, axis=0, keepdims=True))
+        big_b[pl.ds(s, CH, stride=8), :] = dx
+
+    def output(s):
+        lanes = pl.ds(s * 128, 128)
+        outp = dot(wo_t, xbt[:, lanes])
         g = gate[:, lanes]
-        c = cott[:, lanes]
         up_cells = jnp.transpose(g * outp).astype(BF16)
         update[s] = up_cells[0:64]
         update[8 + s] = up_cells[64:128]
-        e = (c * g).astype(BF16)
-        dgp[:, lanes] = (c * outp * g * (1.0 - g)).astype(BF16)
-        dxh = dot(wo[...], e) * gain2c[...]
-        dx = inv * (
-            dxh
-            - jnp.mean(dxh, axis=0, keepdims=True)
-            - xhat * jnp.mean(dxh * xhat, axis=0, keepdims=True)
-        )
-        big_b[pl.ds(s, CH, stride=8), :] = dx
+        dgp[:, lanes] = (cott[:, lanes] * outp * g * (1.0 - g)).astype(BF16)
 
     def received_half(received, big, u):
         big.reshape(CH, 8, 128)[:, 4 * u : 4 * u + 4, :] = received[...].astype(F32)
@@ -345,6 +349,8 @@
             centre(s)
         s3[u] = half_rows(big_b, u)
         dx_here.append(from_cells(5 + u, s3.at[u], r3.at[u]))
+    for s in range(8):
+        output(s)
     update_away = pltpu.make_async_copy(update, update_out, outsem.at[0])
     update_away.start()
     pending.append(update_away.wait)
@@ -373,9 +379,7 @@
         lanes = pl.ds(s * 128, 128)
         d = big[pl.ds(s, CH, stride=8), :]
         sig = sig_ref[:, lanes]
-        dproj[first : first + 128, lanes] = (
-            d * val_ref[:, lanes] * sig * (1.0 - sig)
-        ).astype(BF16)
+        dproj[first : first + 128, lanes] = (d * val_ref[:, lanes]).astype(BF16)
         dproj[first + 128 : first + 256, lanes] = (d * sig).astype(BF16)
 
     def weight_part(n):
@@ -561,12 +565,12 @@
             pltpu.VMEM(message, BF16),
             pltpu.VMEM(by_chip_halves, BF16),
             pltpu.VMEM(by_chip, BF16),
-            pltpu.VMEM(by_chip_halves, BF16),
+            pltpu.VMEM((2, 16, 8, 4, 128), BF16),
             pltpu.VMEM(message_halves, BF16),
             pltpu.VMEM(message_halves, BF16),
             pltpu.VMEM(by_chip_halves, BF16),
-            pltpu.VMEM(by_chip_halves, BF16),
-            pltpu.VMEM(by_chip, BF16),
+            pltpu.VMEM((2, 16, 8, 4, 128), BF16),
+            pltpu.VMEM((16, 8, 8, 128), BF16),
             pltpu.VMEM(message_halves, BF16),
             pltpu.VMEM(message, BF16),
             pltpu.VMEM((2, 128, TOKENS), BF16),
@@ -586,6 +590,8 @@
             pltpu.VMEM((1, 1024), F32),
             pltpu.VMEM(cells, BF16),
             pltpu.VMEM(cells, F32),
+            pltpu.VMEM(cells, F32),
+            pltpu.VMEM(cells, BF16),
             pltpu.VMEM(cells, F32),
             pltpu.VMEM(cells, BF16),
             pltpu.VMEM((4 * CH, 1024), BF16),

time: 76.3 us -> 76.2 us (level)
  no operation moved by 1% of the time
where the time goes in v4:
time: 76.2 us; the launch traced here: 76.1 us
  Pallas kernels  75.4 us (99%)
    pallas_call x1, Pallas kernels, on_device(): pl.pallas_call(kernel, out_shape=(block, block, jax.ShapeDtypeStruct((16,...  73.6 us
    pallas_call x1, Pallas kernels, on_device(): pl.pallas_call(unpack, out_shape=(jax.ShapeDtypeStruct((16, CH), F32), ja...  1.86 us

profile of v4, /device:TPU:1, one launch (start us, length us, event | category | flops | bytes accessed | tf_op | source)
XLA Modules:
  0.0 76.1 jit_solution(4838660590482995540)
XLA Ops:
  0.6 73.6 %shard_map.155 = (bf16[16,64,128]{2,1,0:T(8,128)(2,1)}, bf16[16,64,128]{2,1,0:T(8,128)(2,1)}, f32[16,8,128]{2,1,0:T(8,128)}) custom-call(bf16[16,64,128]{2,1,0:T(8,128)(2,1)} %refs_0_.1, f32[1,128]{1,0:T(1,128)} %bitcast.10, f32[1,128]{1,0:T(1,128)} %bitcast.11, f32[128,512]{1,0:T(8,128)} %refs_3_.1, f32[16,128]{1,0:T(8,128)} %bitcast.8, f32[16,512]{1,0:T(8,128)} %refs_5_.1, ...), custom_call_target="tpu_custom_call" | custom-call | tf_op jit(solution)/shard_map/pallas_call | solution.py:555
  74.2 1.9 %shard_map.156 = (f32[16,128]{1,0:T(8,128)}, f32[16,512]{1,0:T(8,128)}, f32[1,512]{1,0:T(1,128)}, bf16[16,64,128]{2,1,0:T(8,128)(2,1)}, bf16[16,64,128]{2,1,0:T(8,128)(2,1)}) custom-call(f32[16,8,128]{2,1,0:T(8,128)} %get-tuple-element.13.whole_in, bf16[16,64,128]{2,1,0:T(8,128)(2,1)} %get-tuple-element.14.update_in, ...), custom_call_target="tpu_custom_call" | custom-call | tf_op jit(solution)/shard_map/pallas_call | solution.py:618
